TPU v7x, 32 devices: a whole 2x2x4 slice. The times are simulated.
32 devices in a mesh: ha: 2 (over y), az: 16 (over z, x, core).
Axes of the slice: x: 2, y: 2, z: 4, core: 2. Of those that a mesh axis runs over, the one named last changes fastest.
Arguments:
- field: float32 [2, 4096, 8192], P(None, 'ha', 'az'), may hold values from -6 to 6
- terrain: int32 [8192], P('az'), may hold values from 0 to 63
- profile_pick: int32 [8192], P('az'), may hold values from 0 to 15
- profile_table: float32 [16, 4096], replicated, may hold values from -3.140625 to 3.140625
- clutter_mask: int32 [128, 8192], P(None, 'az'), may hold values 0 or 1
- pulse: float32 [63], replicated, may hold values from -0.6 to 0.6
- beam: float32 [31], replicated, may hold values from -0.9 to 0.9
- measured: float32 [2, 128, 8192], P(None, None, 'az'), may hold values from -6 to 6
Outputs:
- field_out: float32 [2, 4096, 8192], P(None, 'ha', 'az')
- sources: float32 [2, 2, 128, 8192], P(None, None, 'ha', 'az')
All inputs are finite; a program needn't handle non-finite values. No bound on the sum of `clutter_mask` on one device may be relied on, other than what follows from the above.
Results may differ from a plain program's by a relative error of at most 0.00022.
Values sent between devices are 32-bit elements; how exact they have to be, the bound alone decides.
A program may use at most 128 MiB of HBM per device.

v0:
```python
import math

import jax
import jax.numpy as jnp
from jax import lax
from jax.sharding import PartitionSpec as P

height_chirp = 1
azimuth_chirp = 3


def broadcast(block, axis, owner):
    block = jnp.where(lax.axis_index(axis) == owner, block, jnp.zeros_like(block))
    return lax.psum(block, axis)


def with_halo(cells, sides, width):
    for axis, dim in sides:
        count = lax.axis_size(axis)
        head = lax.slice_in_dim(cells, 0, width, axis=dim)
        tail = lax.slice_in_dim(cells, cells.shape[dim] - width, cells.shape[dim], axis=dim)
        cells = jnp.concatenate(
            [
                lax.ppermute(tail, axis, [(i, (i + 1) % count) for i in range(count)]),
                cells,
                lax.ppermute(head, axis, [((i + 1) % count, i) for i in range(count)]),
            ],
            axis=dim,
        )
    return cells


def factors(count):
    first = 1
    probe = 1
    while probe * probe <= count:
        if count % probe == 0:
            first = probe
        probe += 1
    return (first, count // first)


def unit_roots(rows, cols, modulus):
    left = lax.broadcasted_iota(jnp.int32, (rows, cols), 0)
    right = lax.broadcasted_iota(jnp.int32, (rows, cols), 1)
    turn = (left * right % modulus).astype(jnp.float32) * (2.0 * math.pi / modulus)
    return (jnp.cos(turn), -jnp.sin(turn))


def chirp_table(first, second, spread, count):
    low = lax.broadcasted_iota(jnp.int32, (first, second), 0)
    high = lax.broadcasted_iota(jnp.int32, (first, second), 1)
    index = low + first * high
    angle = (spread * index * index % (2 * count)).astype(jnp.float32) * (-math.pi / count)
    return (jnp.cos(angle), jnp.sin(angle))


def complex_table(table_re, table_im):
    return jnp.stack([jnp.stack([table_re, -table_im]), jnp.stack([table_im, table_re])])


def cmul(left_re, left_im, right_re, right_im):
    return (left_re * right_re - left_im * right_im, left_re * right_im + left_im * right_re)


def stacked_mul(vals, table_re, table_im):
    new_re, new_im = cmul(vals[0], vals[1], table_re, table_im)
    return jnp.stack([new_re, new_im])


def propagate(part_re, part_im, spread):
    highest = lax.Precision.HIGHEST
    count = part_re.shape[1]
    first, second = factors(count)
    split = (part_re.shape[0], first, second)
    table_shape = (1, first, second)
    outer_re, outer_im = unit_roots(first, first, first)
    inner_re, inner_im = unit_roots(second, second, second)
    twist_re, twist_im = unit_roots(first, second, count)
    twist_re = twist_re.reshape(table_shape)
    twist_im = twist_im.reshape(table_shape)
    phase_re, phase_im = chirp_table(first, second, spread, count)
    phase_re = phase_re.reshape(table_shape)
    phase_im = phase_im.reshape(table_shape)
    outer_fwd = complex_table(outer_re, outer_im)
    inner_fwd = complex_table(inner_re, inner_im)
    inner_inv = complex_table(inner_re.T, -inner_im.T)
    outer_inv = complex_table(outer_re.T, -outer_im.T)
    vals = jnp.stack([part_re.reshape(split), part_im.reshape(split)])
    vals = jnp.einsum("ocka,clab->olkb", outer_fwd, vals, precision=highest)
    vals = stacked_mul(vals, twist_re, twist_im)
    vals = jnp.einsum("clkb,ocbq->olkq", vals, inner_fwd, precision=highest)
    vals = stacked_mul(vals, phase_re, phase_im)
    vals = jnp.einsum("clkq,ocqb->olkb", vals, inner_inv, precision=highest)
    vals = stacked_mul(vals, twist_re, -twist_im)
    vals = jnp.einsum("ocak,clkb->olab", outer_inv, vals, precision=highest)
    scale = 1.0 / count
    return ((vals[0] * scale).reshape(part_re.shape), (vals[1] * scale).reshape(part_im.shape))


def screen_coef(rows, terr, phase, total):
    height = rows.astype(jnp.float32)
    depth = jnp.maximum(height - 0.75 * total, 0.0) / (0.25 * total)
    amount = jnp.exp(-4.0 * depth * depth) * (rows >= terr).astype(jnp.float32)
    return (amount * jnp.cos(phase), amount * jnp.sin(phase))


def onehot_of(picks, count):
    return (picks[None, :] == lax.broadcasted_iota(jnp.int32, (count, picks.shape[0]), 0)).astype(
        jnp.float32
    )


def lookup(table, picks):
    return jnp.einsum(
        "pr,pc->rc", table, onehot_of(picks, table.shape[0]), precision=lax.Precision.HIGHEST
    )


def lookup_cols(table, picks):
    return jnp.einsum(
        "pr,pc->cr", table, onehot_of(picks, table.shape[0]), precision=lax.Precision.HIGHEST
    )


def band(taps, offset):
    hit = offset[:, :, None] == lax.broadcasted_iota(jnp.int32, (1, 1, taps.shape[0]), 2)
    return jnp.sum(jnp.where(hit, taps[None, None, :], 0.0), axis=-1)


def apply_screen(wave, coef):
    new_re, new_im = cmul(wave[0], wave[1], coef[0], coef[1])
    return jnp.stack([new_re, new_im])


def turn_rows(rows):
    new_re, new_im = propagate(rows[0], rows[1], azimuth_chirp)
    return jnp.stack([new_re, new_im])


def turn_items(block):
    return turn_rows(block[:, 0])[:, None]


def to_rows(wave):
    n_az = lax.axis_size("az")
    h_dev = wave.shape[1]
    part_rows = h_dev // n_az
    shaped = wave.reshape(2, n_az, part_rows, wave.shape[2])
    moved = turn_items(lax.all_to_all(shaped, "az", split_axis=1, concat_axis=3, tiled=True))
    return moved.reshape(2, part_rows, moved.shape[3])


def rows_to_slab(rows):
    return lax.all_to_all(rows, "az", split_axis=2, concat_axis=1, tiled=True)


def across(wave):
    return rows_to_slab(to_rows(wave))


def to_tall(wave):
    flipped = jnp.swapaxes(wave, 1, 2)
    return lax.all_to_all(flipped, "ha", split_axis=1, concat_axis=2, tiled=True)


def to_slab(tall):
    flipped = lax.all_to_all(tall, "ha", split_axis=2, concat_axis=1, tiled=True)
    return jnp.swapaxes(flipped, 1, 2)


def down(tall):
    new_re, new_im = propagate(tall[0], tall[1], height_chirp)
    return jnp.stack([new_re, new_im])


def root_strip(wave, bottom):
    return broadcast(wave[:, :bottom, :], "ha", 0)


def beam_forward(values, half_beam, forward_band):
    wider = with_halo(values, (("az", 1),), half_beam)
    return jnp.dot(wider, forward_band, precision=lax.Precision.HIGHEST)


def beam_backward(values, half_beam, back_band):
    wider = with_halo(values, (("az", 1),), half_beam)
    return jnp.dot(wider, back_band, precision=lax.Precision.HIGHEST)


def local(field, terrain, profile_pick, profile_table, clutter_mask, pulse, beam, measured):
    highest = lax.Precision.HIGHEST
    n_slabs = lax.axis_size("ha")
    h_dev = field.shape[1]
    a_dev = field.shape[2]
    total_h = h_dev * n_slabs
    n_cols = a_dev // n_slabs
    slab = lax.axis_index("ha")
    bottom = clutter_mask.shape[0]
    share_rows = bottom // n_slabs
    row_start = slab * share_rows
    mask = clutter_mask.astype(jnp.float32)
    taps_range = pulse.shape[0]
    half_range = (taps_range - 1) // 2
    row_grid = lax.broadcasted_iota(jnp.int32, (bottom, bottom), 0)
    col_grid = lax.broadcasted_iota(jnp.int32, (bottom, bottom), 1)
    rmat = band(pulse, col_grid - row_grid + half_range)
    half_beam = (beam.shape[0] - 1) // 2
    wide = a_dev + 2 * half_beam
    edge = lax.broadcasted_iota(jnp.int32, (wide, a_dev), 0)
    column = lax.broadcasted_iota(jnp.int32, (wide, a_dev), 1)
    forward_band = band(beam, edge - column)
    back_band = band(beam, column - edge + 2 * half_beam)
    slab_rows = slab * h_dev + lax.broadcasted_iota(jnp.int32, (h_dev, 1), 0)
    slab_phase = lookup(
        lax.dynamic_slice_in_dim(profile_table, slab * h_dev, h_dev, 1), profile_pick
    )
    slab_coef = screen_coef(slab_rows, terrain[None, :], slab_phase, total_h)
    steps_count = measured.shape[0]
    wave = field
    result = []
    col_start = slab * n_cols
    tall_rows = lax.broadcasted_iota(jnp.int32, (1, total_h), 1)
    tall_terrain = lax.dynamic_slice_in_dim(terrain, col_start, n_cols, 0)
    tall_pick = lax.dynamic_slice_in_dim(profile_pick, col_start, n_cols, 0)
    tall_coef = screen_coef(
        tall_rows, tall_terrain[:, None], lookup_cols(profile_table, tall_pick), total_h
    )
    layout = "slab"
    tall = wave
    for step in range(steps_count):
        if layout == "slab":
            tall = apply_screen(down(to_tall(across(wave))), tall_coef)
            strip = lax.all_gather(tall[:, :, :bottom], "ha", axis=1, tiled=True)
            strip = jnp.swapaxes(strip, 1, 2)
            layout = "tall"
        else:
            tall_tall = down(tall)
            wave = apply_screen(across(to_slab(tall_tall)), slab_coef)
            strip = root_strip(wave, bottom)
            layout = "slab"
        low_re = strip[0]
        low_im = strip[1]
        power = mask * (low_re * low_re + low_im * low_im)
        target = measured[step]
        ranged = jnp.dot(rmat, power, precision=highest)
        model = beam_forward(ranged, half_beam, forward_band)
        misfit = model - target
        spread_back = beam_backward(misfit, half_beam, back_band)
        back = jnp.einsum("pr,pa->ra", rmat, spread_back, precision=highest)
        whole = jnp.stack([2.0 * mask * low_re * back, 2.0 * mask * low_im * back])
        result.append(lax.dynamic_slice_in_dim(whole, row_start, share_rows, 1))
    return (wave, jnp.stack(result))


def solution(mesh):
    return jax.shard_map(
        local,
        mesh=mesh,
        in_specs=(
            P(None, "ha", "az"),
            P("az"),
            P("az"),
            P(),
            P(None, "az"),
            P(),
            P(),
            P(None, None, "az"),
        ),
        out_specs=(P(None, "ha", "az"), P(None, None, "ha", "az")),
        check_vma=False,
    )
```

profile of v0, /device:TPU:11, one launch (start us, length us, event | category | flops | bytes accessed | tf_op | source)
XLA Modules:
  0.0 1576.4 jit_solution(13658842808562812450)
XLA Ops:
  7.2 8.4 copy.261
  15.6 6.6 all-to-all-start
  23.6 180.9 %all-to-all-done = f32[2,16,128,512]{3,2,0,1:T(8,128)} async-done(((f32[2,16,128,512]{3,2,0,1:T(8,128)}), f32[2,16,128,512]{3,2,0,1:T(8,128)}, u32[]{:S(2)}, u32[]{:S(2)}) %all-to-all-start) | async-done | bytes 8388640 | tf_op jit(solution)/shard_map/all_to_all | solution.py:150
  204.5 6.7 fusion.203
  215.6 4.8 stack_reshape_squeeze.18
  220.4 6.6 copy.263
  231.8 11.3 fusion.71
  246.7 12.7 fusion.46
  266.3 8.8 copy.328
  275.0 11.3 convolution_bitcast_fusion.1
  288.4 8.8 fusion.70
  301.5 5.5 copy.369
  307.0 5.4 copy.370
  312.4 9.3 pad_maximum_fusion.2
  321.7 186.8 %all_to_all.96 = f32[2,128,8192]{1,0,2:T(2,128)S(1)} all-to-all(f32[2,128,8192]{1,0,2:T(2,128)S(1)} %pad_maximum_fusion.2), channel_id=1, replica_groups=mesh['ha'=2,'az'=16] {'az'}, dimensions={2} | all-to-all | bytes 16777216 | tf_op jit(solution)/shard_map/all_to_all | solution.py:155
  512.5 8.8 copy.270
  521.3 13.3 copy.271
  534.6 7.1 all-to-all-start.2
  542.6 91.4 %all-to-all-done.2 = f32[2,512,2048]{2,0,1:T(2,128)} async-done(((f32[2,512,2048]{2,0,1:T(2,128)}), f32[2,512,2048]{2,0,1:T(2,128)}, u32[]{:S(2)}, u32[]{:S(2)}) %all-to-all-start.2) | async-done | bytes 8388640 | tf_op jit(solution)/shard_map/all_to_all | solution.py:164
  634.0 8.2 copy.272
  646.2 5.3 copy.273
  651.5 6.6 copy.275
  658.2 5.5 copy.274
  668.4 8.2 fusion.69
  679.5 13.0 fusion.52
  693.9 8.5 fusion.55
  702.4 5.0 copy.423
  708.9 8.7 fusion.68
  725.3 5.8 copy.285
  731.1 6.6 copy.286
  737.7 5.6 copy.287
  743.3 21.6 %multiply_subtract_fusion.6 = (f32[256,4096]{1,0:T(8,128)}, f32[256,4096]{1,0:T(8,128)}) fusion(f32[256,4096]{1,0:T(8,128)} %copy.287, f32[256,4096]{1,0:T(8,128)} %copy.285, f32[4096]{0:T(1024)S(1)} %multiply_exponential_fusion, s32[256]{0:T(256)S(1)} %dynamic_slice.15, f32[16,4096]{1,0:T(8,128)S(1)} %copy-done, s32[256]{0:T(256)S(1)} %dynamic_slice.16), kind=kOutput, calls=%fused_computation.104 | convolution fusion | flops 211816448 | bytes 17057792 | tf_op jit(solution)/shard_map/pr,pc->cr/dot_general | solution.py:121
  764.9 5.6 copy.288
  770.5 6.6 copy.292
  777.1 6.0 copy.291
  787.9 8.2 fusion.67
  798.9 12.9 fusion.58
  813.3 8.5 fusion.61
  821.8 5.0 copy.422
  828.3 8.7 fusion.66
  844.5 20.8 %copy.301 = f32[2,256,4096]{1,0,2:T(2,128)S(1)} copy(f32[2,256,4096]{1,2,0:T(8,128)S(1)} %pad_maximum_fusion.7) | data formatting | bytes 16777216 | tf_op jit(solution)/shard_map/stack | solution.py:174
  865.3 94.3 %all_to_all.97 = f32[2,256,4096]{1,0,2:T(2,128)S(1)} all-to-all(f32[2,256,4096]{1,0,2:T(2,128)S(1)} %copy.301), channel_id=1, replica_groups=mesh['ha'=2,'az'=16] {'ha'}, dimensions={2} | all-to-all | bytes 16777216 | tf_op jit(solution)/shard_map/all_to_all | solution.py:168
  963.7 8.8 copy.303
  972.5 8.7 copy.304
  985.5 189.4 %all_to_all.98 = f32[2,16,128,512]{3,2,0,1:T(8,128)S(1)} all-to-all(f32[2,16,128,512]{3,2,0,1:T(8,128)S(1)} %copy.305), channel_id=1, replica_groups=mesh['ha'=2,'az'=16] {'az'}, dimensions={1} | all-to-all | bytes 16777216 | tf_op jit(solution)/shard_map/all_to_all | solution.py:150
  1182.6 4.8 stack_reshape_squeeze.22
  1187.3 6.6 copy.307
  1198.7 11.0 fusion.65
  1213.5 12.8 fusion.49
  1233.1 8.8 copy.351
  1241.9 11.5 convolution_bitcast_fusion
  1255.4 8.8 fusion.64
  1268.6 5.4 copy.374
  1274.0 5.5 copy.375
  1279.5 10.1 pad_maximum_fusion.9
  1289.5 5.8 all-to-all-start.5
  1296.4 6.8 select_reduce_fusion.1
  1304.2 8.3 all_gather.3
  1316.1 162.3 %all-to-all-done.5 = f32[2,128,8192]{1,0,2:T(2,128)} async-done(((f32[2,128,8192]{1,0,2:T(2,128)}), f32[2,128,8192]{1,0,2:T(2,128)}, u32[]{:S(2)}, u32[]{:S(2)}) %all-to-all-start.5) | async-done | bytes 8388640 | tf_op jit(solution)/shard_map/all_to_all | solution.py:155
  1478.4 8.2 copy.421
  1487.4 19.1 %fusion.43 = (f32[1,2048,512]{1,2,0:T(8,128)S(1)}, f32[1,2048,512]{1,2,0:T(8,128)S(1)}) fusion(f32[64,8,16,128]{3,2,1,0:T(8,128)S(1)} %bitcast.378, f32[64,8,16,128]{3,2,1,0:T(8,128)S(1)} %bitcast.377, f32[2048]{0:T(1024)S(1)} %multiply_exponential_fusion.1, s32[2048]{0:T(1024)S(1)} %iota_add_fusion, s32[512]{0:T(512)S(1)} %copy-done.30, ...), kind=kOutput, calls=%fused_computation.78 | convolution fusion | flops 211820544 | bytes 16928772 | tf_op jit(solution)/shard_map/pr,pc->rc/dot_general | solution.py:115
  1523.6 14.5 all-reduce.2.cloned.1.call-done
  1548.6 7.9 pad_maximum_fusion
  1556.5 8.7 copy.323
  (174 shorter events, 147.6 us)
Async XLA Ops:
  7.2 736.1 %copy-start = (f32[16,4096]{1,0:T(8,128)S(1)}, f32[16,4096]{1,0:T(8,128)}, u32[]{:S(2)}) copy-start(f32[16,4096]{1,0:T(8,128)} %param.11) | copy-start | bytes 786436
  15.6 188.9 %all-to-all-start = ((f32[2,16,128,512]{3,2,0,1:T(8,128)}), f32[2,16,128,512]{3,2,0,1:T(8,128)}, u32[]{:S(2)}, u32[]{:S(2)}) async-start(f32[2,16,128,512]{3,2,0,1:T(8,128)} %copy.261), calls=%async_computation | async-start | bytes 16777216 | tf_op jit(solution)/shard_map/all_to_all | solution.py:150
  22.3 264.1 %copy-start.20 = (f32[64,128]{1,0:T(8,128)}, f32[64,128]{1,0:T(8,128)S(1)}, u32[]{:S(2)}) copy-start(f32[64,128]{1,0:T(8,128)S(1)} %fusion.170) | copy-start | bytes 98308
  23.0 220.0 %copy-start.22 = (f32[64,128]{1,0:T(8,128)}, f32[64,128]{1,0:T(8,128)S(1)}, u32[]{:S(2)}) copy-start(f32[64,128]{1,0:T(8,128)S(1)} %get-tuple-element.93) | copy-start | bytes 98308
  23.0 263.3 %copy-start.18 = (f32[64,128]{1,0:T(8,128)}, f32[64,128]{1,0:T(8,128)S(1)}, u32[]{:S(2)}) copy-start(f32[64,128]{1,0:T(8,128)S(1)} %get-tuple-element.92) | copy-start | bytes 98308
  23.4 223.3 %copy-start.13 = (f32[1,2,128,128]{2,3,1,0:T(8,128)}, f32[1,2,128,128]{2,3,1,0:T(8,128)S(1)}, u32[]{:S(2)}) copy-start(f32[1,2,128,128]{2,3,1,0:T(8,128)S(1)} %get-tuple-element.75) | copy-start | bytes 393220
  23.4 223.3 %copy-start.15 = (f32[1,2,128,128]{2,3,1,0:T(8,128)}, f32[1,2,128,128]{2,3,1,0:T(8,128)S(1)}, u32[]{:S(2)}) copy-start(f32[1,2,128,128]{2,3,1,0:T(8,128)S(1)} %get-tuple-element.82) | copy-start | bytes 393220
  23.4 251.6 %copy-start.9 = (f32[1,2,128,128]{2,3,1,0:T(8,128)}, f32[1,2,128,128]{2,3,1,0:T(8,128)S(1)}, u32[]{:S(2)}) copy-start(f32[1,2,128,128]{2,3,1,0:T(8,128)S(1)} %get-tuple-element.74) | copy-start | bytes 393220
  23.4 251.6 %copy-start.11 = (f32[1,2,128,128]{2,3,1,0:T(8,128)}, f32[1,2,128,128]{2,3,1,0:T(8,128)S(1)}, u32[]{:S(2)}) copy-start(f32[1,2,128,128]{2,3,1,0:T(8,128)S(1)} %get-tuple-element.83) | copy-start | bytes 393220
  23.6 235.9 %copy-start.24 = (f32[64,128]{1,0:T(8,128)}, f32[64,128]{1,0:T(8,128)S(1)}, u32[]{:S(2)}) copy-start(f32[64,128]{1,0:T(8,128)S(1)} %get-tuple-element.88) | copy-start | bytes 98308
  23.6 235.9 %copy-start.26 = (f32[64,128]{1,0:T(8,128)}, f32[64,128]{1,0:T(8,128)S(1)}, u32[]{:S(2)}) copy-start(f32[64,128]{1,0:T(8,128)S(1)} %get-tuple-element.89) | copy-start | bytes 98308
  534.6 7.1 copy-start.29
  534.6 7.2 copy-start.33
  534.6 99.4 %all-to-all-start.2 = ((f32[2,512,2048]{2,0,1:T(2,128)}), f32[2,512,2048]{2,0,1:T(2,128)}, u32[]{:S(2)}, u32[]{:S(2)}) async-start(f32[2,512,2048]{2,0,1:T(2,128)} %copy.271), calls=%async_computation.2 | async-start | bytes 16777216 | tf_op jit(solution)/shard_map/all_to_all | solution.py:164
  663.7 4.8 copy-start.4
  783.1 4.8 copy-start.5
  1198.7 11.0 copy-start.19
  1198.7 11.0 copy-start.23
  1211.8 1.7 copy-start.14
  1211.8 1.7 copy-start.16
  1213.5 12.8 copy-start.25
  1213.5 12.8 copy-start.27
  1233.0 8.8 copy-start.10
  1233.1 8.8 copy-start.12
  1241.9 11.5 copy-start.21
  1289.5 5.9 copy-start.28
  1289.5 6.4 copy-start.35
  1289.5 6.9 copy-start.36
  1289.5 188.9 %all-to-all-start.5 = ((f32[2,128,8192]{1,0,2:T(2,128)}), f32[2,128,8192]{1,0,2:T(2,128)}, u32[]{:S(2)}, u32[]{:S(2)}) async-start(f32[2,128,8192]{1,0,2:T(2,128)} %pad_maximum_fusion.9), calls=%async_computation.5 | async-start | bytes 16777216 | tf_op jit(solution)/shard_map/all_to_all | solution.py:155
  1295.4 242.7 %all-reduce.2.cloned.1.call-start = ((), (), s32[]{:S(2)}) async-start(), calls=%async_computation.6 | async-start | bytes 1048576 | tf_op jit(solution)/shard_map/psum | solution.py:14
  1295.6 7.7 copy-start.1
  1296.4 16.1 %copy-start.6 = (f32[128,128]{1,0:T(8,128)}, f32[128,128]{1,0:T(8,128)S(1)}, u32[]{:S(2)}) copy-start(f32[128,128]{1,0:T(8,128)S(1)} %select_reduce_fusion.2) | copy-start | bytes 196612
  1313.0 0.7 copy-start.8
  1313.7 197.1 %collective-permute-start = (f32[128,15]{1,0:T(8,128)S(1)}, f32[128,15]{1,0:T(8,128)S(1)}, u32[]{:S(2)}, u32[]{:S(2)}) collective-permute-start(f32[128,15]{1,0:T(8,128)S(1)} %get-tuple-element.68), channel_id=1, source_target_pairs={{0,1},{1,2},{2,3},{3,4},{4,5},{5,6},{6,7},{7,8},{8,9},{9,10},{10,1... | collective-permute-start | bytes 23048 | tf_op jit(solution)/shard_map/ppermute | solution.py:24
  1315.9 194.9 %collective-permute-start.1 = (f32[128,15]{1,0:T(8,128)S(1)}, f32[128,15]{1,0:T(8,128)S(1)}, u32[]{:S(2)}, u32[]{:S(2)}) collective-permute-start(f32[128,15]{1,0:T(8,128)S(1)} %get-tuple-element.69), channel_id=1, source_target_pairs={{1,0},{2,1},{3,2},{4,3},{5,4},{6,5},{7,6},{8,7},{9,8},{10,9},{11,1... | collective-permute-start | bytes 23048 | tf_op jit(solution)/shard_map/ppermute | solution.py:26
  1486.7 0.7 copy-start.30
  1486.7 0.7 copy-start.34
  1506.5 2.1 copy-start.2
  1506.5 3.4 copy-start.3
  1510.8 0.6 copy-start.31
  1511.4 0.6 copy-start.32
  1514.8 3.1 collective-permute-start.2
  1516.2 4.9 collective-permute-start.3
  1539.7 4.1 collective-permute-start.4
  1541.5 4.6 collective-permute-start.5
  1548.0 17.2 %collective-permute-start.6 = (f32[128,15]{1,0:T(8,128)S(1)}, f32[128,15]{1,0:T(8,128)S(1)}, u32[]{:S(2)}, u32[]{:S(2)}) collective-permute-start(f32[128,15]{1,0:T(8,128)S(1)} %get-tuple-element.70), channel_id=1, source_target_pairs={{0,1},{1,2},{2,3},{3,4},{4,5},{5,6},{6,7},{7,8},{8,9},{9,10},{10,1... | collective-permute-start | bytes 23048 | tf_op jit(solution)/shard_map/ppermute | solution.py:24
  1548.4 16.8 %collective-permute-start.7 = (f32[128,15]{1,0:T(8,128)S(1)}, f32[128,15]{1,0:T(8,128)S(1)}, u32[]{:S(2)}, u32[]{:S(2)}) collective-permute-start(f32[128,15]{1,0:T(8,128)S(1)} %get-tuple-element.71), channel_id=1, source_target_pairs={{1,0},{2,1},{3,2},{4,3},{5,4},{6,5},{7,6},{8,7},{9,8},{10,9},{11,1... | collective-permute-start | bytes 23048 | tf_op jit(solution)/shard_map/ppermute | solution.py:26
  1556.5 9.7 copy-start.7
  1556.5 9.7 copy-start.17
Sparse Core Ops, SparseCore 0:
  1510.9 27.1 all-reduce.1
where the time goes:
time: 1590 us; the launch traced here: 1580 us
  blocking collectives  479 us (30%)
  waiting for transfers between devices  456 us (29%)
  local copies, waits for them, and re-layouts  291 us (18%)
  matrix products  219 us (14%)
  other arithmetic  90.2 us (6%)
  starting transfers between devices  25.7 us (2%)
    all_to_all x1, blocking collectives, to_rows(): lax.all_to_all(shaped, 'az', split_axis=1, concat_axis=3, tiled=True)  189 us
    all_to_all x1, blocking collectives, rows_to_slab(): return lax.all_to_all(rows, 'az', split_axis=2, concat_axis=1, tiled=True)  187 us
    all_to_all x1, waiting for transfers between devices, to_rows(): lax.all_to_all(shaped, 'az', split_axis=1, concat_axis=3, tiled=True)  181 us
    all_to_all x1, waiting for transfers between devices, rows_to_slab(): return lax.all_to_all(rows, 'az', split_axis=2, concat_axis=1, tiled=True)  162 us
    all_to_all x1, blocking collectives, to_slab(): lax.all_to_all(tall, 'ha', split_axis=2, concat_axis=1, tiled=True)  94.3 us
    all_to_all x1, waiting for transfers between devices, to_tall(): lax.all_to_all(flipped, 'ha', split_axis=1, concat_axis=2, tiled=True)  91.4 us
    dot_general x4, matrix products, propagate(): vals = jnp.einsum('clkb,ocbq->olkq', vals, inner_fwd, precision=highest)  51.4 us
    another operation x8, local copies, waits for them, and re-layouts, propagate(): vals = jnp.stack([part_re.reshape(split), part_im.reshape(split)])  41.8 us
  transfers between devices with their start and end apart: 12, of which 7 were waited for; matrix products, arithmetic and copies ran while one was open for 4% of the time, Pallas kernels for 0%

commit v1 on v0

v1 whole, which is shorter than its diff:
```python
import math

import jax
import jax.numpy as jnp
import numpy as np
from jax import lax
from jax.sharding import PartitionSpec as P

height_chirp = 1
azimuth_chirp = 3
EXACT = lax.Precision.HIGHEST
FAST = lax.Precision.HIGH


def iota(shape, dim):
    return lax.broadcasted_iota(jnp.int32, shape, dim)


def cmul(left, right):
    return (left[0] * right[0] - left[1] * right[1], left[0] * right[1] + left[1] * right[0])


def turn(amount, period, scale=1.0):
    angle = (amount % period).astype(jnp.float32) * (2.0 * math.pi / period)
    return (scale * jnp.cos(angle), scale * jnp.sin(angle))


def inverse_of(spread, count):
    return pow(spread, -1, 2 * count)


def gauss(spread, count):
    index = np.arange(count, dtype=np.int64)
    angle = (spread * index * index % (2 * count)) * (-math.pi / count)
    return (float(np.sum(np.cos(angle))) / count, float(np.sum(np.sin(angle))) / count)


def chirp(index, spread, count):
    return turn(index * index % (2 * count) * inverse_of(spread, count), 2 * count)


def roots(size, spread, count):
    amount = iota((size, size), 0) * iota((size, size), 1) % size * (inverse_of(spread, count) % size)
    re, im = turn(-amount, size)
    return jnp.stack([jnp.stack([re, -im]), jnp.stack([im, re])])


def twist(rows, cols, spread, count):
    left, right = iota((rows, cols), 0), iota((rows, cols), 1)
    return turn(-(left * right % count * (inverse_of(spread, count) % count)), count)


def band(taps, offset):
    hit = offset[:, :, None] == lax.broadcasted_iota(jnp.int32, (1, 1, taps.shape[0]), 2)
    return jnp.sum(jnp.where(hit, taps[None, None, :], 0.0), axis=-1)


def damping(rows, total):
    depth = jnp.maximum(rows.astype(jnp.float32) - 0.75 * total, 0.0) / (0.25 * total)
    return jnp.exp(-4.0 * depth * depth)


def onehot_of(picks, count):
    return (picks[None] == iota((count,) + picks.shape, 0)).astype(jnp.float32)


def halo(cells, width, axis="az"):
    count = lax.axis_size(axis)
    head = cells[..., :width]
    tail = cells[..., cells.shape[-1] - width:]
    left = lax.ppermute(tail, axis, [(i, (i + 1) % count) for i in range(count)])
    right = lax.ppermute(head, axis, [((i + 1) % count, i) for i in range(count)])
    return left, right


def local(field, terrain, profile_pick, profile_table, clutter_mask, pulse, beam, measured):
    n_ha = lax.axis_size("ha")
    n_az = lax.axis_size("az")
    n_dev = n_ha * n_az
    slab = lax.axis_index("ha")
    block = lax.axis_index("az")
    place = block * n_ha + slab
    both = ("az", "ha")
    h_dev, a_dev = field.shape[1], field.shape[2]
    total_h, total_a = h_dev * n_ha, a_dev * n_az
    cols = a_dev // n_ha
    bottom = clutter_mask.shape[0]
    h_first = max(64, n_dev)
    h_second = total_h // h_first
    own = h_first // n_dev
    n_prof = profile_table.shape[0]

    taps_range = pulse.shape[0]
    half_range = (taps_range - 1) // 2
    half_beam = (beam.shape[0] - 1) // 2
    reach = 2 * half_beam
    wide = a_dev + 2 * reach
    middle = a_dev + 2 * half_beam
    share = bottom // n_ha
    rmat = band(pulse, iota((bottom, bottom), 1) - iota((bottom, bottom), 0) + half_range)
    forward_band = band(beam, iota((wide, middle), 0) - iota((wide, middle), 1))
    back_band = band(beam, iota((middle, a_dev), 1) - iota((middle, a_dev), 0) + reach)
    own_rmat = lax.dynamic_slice_in_dim(rmat, slab * share, share, 1)
    mask = clutter_mask.astype(jnp.float32)
    left, right = halo(mask, reach)
    wide_mask = jnp.concatenate([left, mask, right], axis=1)
    left, right = halo(measured, half_beam)
    wide_measured = jnp.concatenate([left, measured, right], axis=2)

    def sources_of(low_re, low_im, step):
        power = wide_mask * (low_re * low_re + low_im * low_im)
        ranged = jnp.dot(rmat, power, precision=EXACT)
        misfit = jnp.dot(ranged, forward_band, precision=EXACT) - wide_measured[step]
        spread_back = jnp.dot(misfit, back_band, precision=EXACT)
        back = jnp.einsum("pr,pa->ra", own_rmat, spread_back, precision=EXACT)
        weight = 2.0 * lax.dynamic_slice_in_dim(mask, slab * share, share, 0) * back
        mine = [
            lax.dynamic_slice(low, (slab * share, reach), (share, a_dev)) for low in (low_re, low_im)
        ]
        return jnp.stack([weight * mine[0], weight * mine[1]])

    all_pick = lax.all_gather(profile_pick, "az", tiled=True)
    all_terrain = lax.all_gather(terrain, "az", tiled=True)
    height = iota((1, total_h), 1)
    z_chirp = chirp(height, height_chirp, total_h)
    z_gain = gauss(height_chirp, total_h)
    y_gain = gauss(azimuth_chirp, total_a)
    gain = (z_gain[0] * y_gain[0] - z_gain[1] * y_gain[1], z_gain[0] * y_gain[1] + z_gain[1] * y_gain[0])
    amount = damping(height, total_h)
    bend = cmul((amount * jnp.cos(profile_table), amount * jnp.sin(profile_table)), cmul(z_chirp, gain))
    bend_again = cmul(bend, z_chirp)

    slab_z = chirp(slab * h_dev + iota((h_dev, 1), 0), height_chirp, total_h)
    block_y = chirp(block * a_dev + iota((1, a_dev), 1), azimuth_chirp, total_a)
    start = cmul((field[0], field[1]), cmul(slab_z, block_y))
    start = jnp.stack(start).reshape(2, h_dev, n_ha, cols).transpose(2, 0, 1, 3)

    w_first = roots(h_first, height_chirp, total_h)
    w_second = roots(h_second, height_chirp, total_h)
    tw_re, tw_im = (t[:, :, None] for t in twist(h_first, h_second, height_chirp, total_h))
    tall = lax.all_to_all(start, "ha", split_axis=0, concat_axis=0)
    tall = tall.reshape(n_ha, 2, h_first // n_ha, h_second, cols)
    w_in = w_first.reshape(2, 2, h_first, n_ha, h_first // n_ha)
    tall = jnp.einsum("ocksa,scabq->okbq", w_in, tall, precision=FAST)
    tall = jnp.stack(cmul(tall, (tw_re, tw_im)))
    tall = jnp.einsum("ocjb,ckbq->kojq", w_second, tall, precision=FAST)
    tall = tall.reshape(n_dev, own, 2, h_second, cols)
    rows = lax.all_to_all(tall, both, split_axis=0, concat_axis=0)

    w_blocks = roots(n_dev, azimuth_chirp, total_a)
    w_cols = roots(cols, azimuth_chirp, total_a)
    ty_re, ty_im = (t[:, None, None, :] for t in twist(n_dev, cols, azimuth_chirp, total_a))
    rows = jnp.einsum("ocnp,pucjq->onujq", w_blocks, rows, precision=FAST)
    rows = jnp.stack(cmul(rows, (ty_re, ty_im)))
    rows = jnp.einsum("ocmq,cnujq->onujm", w_cols, rows, precision=FAST)

    def own_rows(table):
        table = table.reshape(n_prof, h_second, n_dev, own)
        table = lax.dynamic_slice_in_dim(table, place, 1, 2)[:, :, 0]
        return jnp.swapaxes(table, 1, 2)

    own_first = place * own + iota((1, own, 1, 1), 1)
    own_height = own_first + h_first * iota((1, 1, h_second, 1), 2)
    grid_pick = all_pick.reshape(cols, n_dev).T
    grid_terrain = all_terrain.reshape(cols, n_dev).T
    hot = onehot_of(grid_pick, n_prof)
    azimuth = iota((n_dev, cols), 0) + n_dev * iota((n_dev, cols), 1)
    y_chirp = chirp(azimuth, azimuth_chirp, total_a)
    ground = (own_height >= grid_terrain[:, None, None, :]).astype(jnp.float32)
    y_turn = tuple(t[:, None, None, :] for t in cmul(y_chirp, y_chirp))
    bent = tuple(
        ground * jnp.einsum("fuj,fnm->nujm", own_rows(t), hot, precision=FAST) for t in bend_again
    )
    next_rows = jnp.stack(cmul(rows, cmul(bent, y_turn)))

    n_low = -(-bottom // h_first)
    low_bend = tuple(
        ground[:, :, :n_low]
        * jnp.einsum("fuj,fnm->nujm", own_rows(t)[:, :, :n_low], hot, precision=EXACT)
        for t in bend
    )
    low_chirp = tuple(t[:, None, None, :] for t in y_chirp)
    low = jnp.stack(cmul(rows[:, :, :, :n_low], cmul(low_bend, low_chirp)))
    low = low.transpose(0, 2, 3, 4, 1).reshape(2, own, n_low, total_a)
    low = jnp.concatenate([low[..., total_a - reach:], low, low[..., :reach]], axis=-1)
    if bottom % h_first == 0:
        windows = jnp.stack([low[..., i * a_dev:i * a_dev + wide] for i in range(n_az)])
        windows = lax.all_to_all(windows, "az", split_axis=0, concat_axis=0)
        windows = lax.all_gather(windows, "ha")
        windows = windows.transpose(2, 4, 1, 0, 3, 5).reshape(2, bottom, wide)
    else:
        spread = jnp.zeros((2, h_first, n_low, low.shape[-1]), jnp.float32)
        spread = lax.dynamic_update_slice_in_dim(spread, low, place * own, 1)
        spread = jnp.swapaxes(spread, 1, 2).reshape(2, n_low * h_first, low.shape[-1])
        spread = lax.psum(spread[:, :bottom], both)
        windows = lax.dynamic_slice_in_dim(spread, block * a_dev, wide, 2)
    first_sources = sources_of(windows[0], windows[1], 0)

    rows = jnp.einsum("ocqm,cnujm->onujq", w_cols, next_rows, precision=FAST)
    rows = jnp.stack(cmul(rows, (ty_re, ty_im)))
    rows = jnp.einsum("ocpn,cnujq->puojq", w_blocks, rows, precision=FAST)
    tall = lax.all_to_all(rows, both, split_axis=0, concat_axis=0)
    tall = tall.reshape(h_first, 2, h_second, cols)
    tall = jnp.einsum("ocbj,kcjq->okbq", w_second, tall, precision=FAST)
    tall = jnp.stack(cmul(tall, (tw_re, tw_im)))
    tall = jnp.einsum("ocak,ckbq->oabq", w_first, tall, precision=FAST)
    tall = tall.reshape(2, total_h, cols)

    col_start = slab * cols
    tall_pick = lax.dynamic_slice_in_dim(profile_pick, col_start, cols, 0)
    tall_terrain = lax.dynamic_slice_in_dim(terrain, col_start, cols, 0)
    tall_hot = onehot_of(tall_pick, n_prof)
    tall_ground = (iota((total_h, 1), 0) >= tall_terrain[None, :]).astype(jnp.float32)
    tall_y = chirp(block * a_dev + col_start + iota((1, cols), 1), azimuth_chirp, total_a)
    tall_bent = tuple(
        tall_ground * jnp.einsum("fh,fq->hq", t, tall_hot, precision=FAST) for t in bend
    )
    last = jnp.stack(cmul(tall, cmul(tall_bent, tall_y)))

    strip = lax.all_gather(last[:, :bottom], "ha", axis=2, tiled=True)
    left, right = halo(strip, reach)
    strip = jnp.concatenate([left, strip, right], axis=2)
    second_sources = sources_of(strip[0], strip[1], 1)

    out = last.reshape(2, n_ha, h_dev, cols).transpose(1, 0, 2, 3)
    out = lax.all_to_all(out, "ha", split_axis=0, concat_axis=0)
    out = out.transpose(1, 2, 0, 3).reshape(2, h_dev, a_dev)
    return (out, jnp.stack([first_sources, second_sources]))


def solution(mesh):
    return jax.shard_map(
        local,
        mesh=mesh,
        in_specs=(
            P(None, "ha", "az"),
            P("az"),
            P("az"),
            P(),
            P(None, "az"),
            P(),
            P(),
            P(None, None, "az"),
        ),
        out_specs=(P(None, "ha", "az"), P(None, None, "ha", "az")),
        check_vma=False,
    )
```

time: 1590 us -> 862 us (0.54)
  waiting for transfers between devices: 456 us -> 247 us
  local copies, waits for them, and re-layouts: 291 us -> 112 us
  blocking collectives: 479 us -> 312 us
  matrix products: 219 us -> 92.7 us
  other arithmetic: 90.2 us -> 42.3 us
  starting transfers between devices: 25.7 us -> 44.5 us
    all_to_all x3 -> x0, blocking collectives: 471 us -> none  [the longest x1 189 us: to_rows(): lax.all_to_all(shaped, 'az', split_axis=1, concat_axis=3, tiled=True)]
    all_gather x1 -> x4, blocking collectives: 8.31 us -> 312 us  [the longest x1 193 us: local(): all_terrain = lax.all_gather(terrain, 'az', tiled=True)]
    all_to_all x3 -> x5, waiting for transfers between devices: 435 us -> 241 us  [the longest x1 150 us: local(): tall = lax.all_to_all(rows, both, split_axis=0, concat_axis=0)]
    dot_general x26 -> x22, matrix products: 219 us -> 92.7 us  [the longest x1 12.4 us: local(): rows = jnp.einsum('ocnp,pucjq->onujq', w_blocks, rows, precision=FAST)]
    another operation x11 -> x0, local copies, waits for them, and re-layouts: 80.1 us -> none  [the longest x8 41.8 us: propagate(): vals = jnp.stack([part_re.reshape(split), part_im.reshape(split)])]
    mul x10 -> x0, local copies, waits for them, and re-layouts: 49.5 us -> none  [the longest x5 25.9 us: propagate(): vals[1] * scale]
    another operation x16 -> x11, other arithmetic: 43.5 us -> 5.88 us  [the longest x1 1.65 us: local(): rows = jnp.stack(cmul(rows, (ty_re, ty_im)))]
    slice x14 -> x12, local copies, waits for them, and re-layouts: 48.4 us -> 19 us  [the longest x1 7.82 us: local(): start = cmul((field[0], field[1]), cmul(slab_z, block_y))]
  transfers between devices with their start and end apart: 12 -> 11, of which waited for: 7 -> 4; matrix products, arithmetic and copies ran while one was open for 4% -> 11% of each run, Pallas kernels for 0% -> 0%
where the time goes in v1:
time: 862 us; the launch traced here: 852 us
  blocking collectives  312 us (36%)
  waiting for transfers between devices  247 us (29%)
  local copies, waits for them, and re-layouts  112 us (13%)
  matrix products  92.7 us (11%)
  starting transfers between devices  44.5 us (5%)
  other arithmetic  42.3 us (5%)
    all_gather x1, blocking collectives, local(): all_terrain = lax.all_gather(terrain, 'az', tiled=True)  193 us
    all_to_all x1, waiting for transfers between devices, local(): tall = lax.all_to_all(rows, both, split_axis=0, concat_axis=0)  150 us
    all_gather x1, blocking collectives, local(): windows = lax.all_gather(windows, 'ha')  94.8 us
    all_to_all x1, waiting for transfers between devices, local(): tall = lax.all_to_all(start, 'ha', split_axis=0, concat_axis=0)  91 us
    unnamed x64, local copies, waits for them, and re-layouts  25.7 us
  transfers between devices with their start and end apart: 11, of which 4 were waited for; matrix products, arithmetic and copies ran while one was open for 11% of the time, Pallas kernels for 0%

profile of v1, /device:TPU:11, one launch (start us, length us, event | category | flops | bytes accessed | tf_op | source)
XLA Modules:
  0.0 851.7 jit_solution(14552208076960139999)
XLA Ops:
  0.8 7.8 fusion.200
  8.6 5.4 copy.245
  14.0 5.3 copy.246
  19.4 4.5 multiply_subtract_fusion.6
  24.9 4.0 copy.176
  28.9 7.0 all-to-all-start
  36.7 91.0 %all-to-all-done = f32[2,2,2048,256]{2,3,1,0:T(8,128)} async-done(((f32[2,2,2048,256]{2,3,1,0:T(8,128)}), f32[2,2,2048,256]{2,3,1,0:T(8,128)}, u32[]{:S(2)}, u32[]{:S(2)}) %all-to-all-start) | async-done | bytes 8388640 | tf_op jit(solution)/shard_map/all_to_all | solution.py:141
  127.6 8.7 %copy.177 = f32[2,2,2048,256]{3,2,1,0:T(8,128)} copy(f32[2,2,2048,256]{2,3,1,0:T(8,128)} %all-to-all-done) | data formatting | bytes 16777216 | tf_op jit(solution)/shard_map/all_to_all | solution.py:141
  136.3 12.0 %fusion.25 = f32[2,64,64,256]{3,1,2,0:T(8,128)S(1)} fusion(f32[2,2,32,64,256]{4,3,2,1,0:T(8,128)} %bitcast.393, f32[1,1,64,2,32]{2,4,3,1,0:T(8,128)S(1)} %get-tuple-element.57, f32[1,1,64,2,32]{2,4,3,1,0:T(8,128)S(1)} %get-tuple-element.56, f32[1,1,64,2,32]{2,4,3,1,0:T(8,128)S(1)} %get-tuple-element.55), kind=kOutput, calls=%fused_computation.64 | convolution fusion | flops 1610661888 | bytes 16826368 | tf_op jit(solution)/shard_map/ocksa,scabq->okbq/dot_general | solution.py:144
  148.3 1.9 multiply_subtract_fusion.5
  151.4 8.5 fusion.10
  159.8 7.6 copy.180
  167.5 6.3 all-to-all-start.1
  173.8 192.9 %all-gather.1 = s32[16,1,512]{2,1,0:T(1,128)S(1)} all-gather(s32[1,1,512]{2,1,0:T(1,128)S(1)} %bitcast.409), channel_id=1, replica_groups=mesh['ha'=2,'az'=16] {'az'}, dimensions={0}, use_global_device_ids=true | all-gather | bytes 34816 | tf_op jit(solution)/shard_map/all_gather | solution.py:123
  366.9 16.4 %all-gather.2 = s32[16,1,512]{2,1,0:T(1,128)S(1)} all-gather(s32[1,1,512]{2,1,0:T(1,128)S(1)} %bitcast.410), channel_id=1, replica_groups=mesh['ha'=2,'az'=16] {'az'}, dimensions={0}, use_global_device_ids=true | all-gather | bytes 34816 | tf_op jit(solution)/shard_map/all_gather | solution.py:122
  385.1 1.9 copy.188
  388.0 1.9 copy.186
  393.8 3.3 fusion.44
  397.1 12.4 %fusion.34 = f32[2,32,2,64,256]{4,1,3,2,0:T(8,128)S(1)} fusion(f32[32,2,2,64,256]{4,2,3,1,0:T(2,128)} %all-to-all-done.1, f32[1,2,32,32]{3,2,1,0:T(8,128)S(1)} %get-tuple-element.50, f32[1,2,32,32]{3,2,1,0:T(8,128)S(1)} %get-tuple-element.49), kind=kOutput, calls=%fused_computation.68 | convolution fusion | flops 805310464 | bytes 16793600 | tf_op jit(solution)/shard_map/ocnp,pucjq->onujq/dot_general | solution.py:153
  409.4 2.0 multiply_subtract_fusion.4
  411.5 1.7 maximum_bitcast_fusion.2
  413.1 11.6 %fusion.19 = f32[2,32,2,64,256]{4,3,0,2,1:T(8,128)S(1)} fusion(f32[2,32,2,64,256,1]{4,1,3,2,0,5:T(8,128)S(1)} %maximum_bitcast_fusion.2, f32[1,2,256,256]{3,2,1,0:T(8,128)S(1)} %get-tuple-element.42, f32[1,2,256,256]{3,2,1,0:T(8,128)S(1)} %get-tuple-element.41), kind=kOutput, calls=%fused_computation.62 | convolution fusion | flops 6442713088 | bytes 17825792 | tf_op jit(solution)/shard_map/ocmq,cnujq->onujm/dot_general | solution.py:155
  424.8 3.3 subtract_bitcast_fusion
  429.2 11.4 %fusion.22 = f32[2,32,2,64,256]{4,1,3,2,0:T(8,128)S(1)} fusion(f32[2,32,2,64,256,1]{4,3,2,1,0,5:T(8,128)S(1)} %maximum_bitcast_fusion.3, f32[1,2,256,256]{3,2,1,0:T(8,128)S(1)} %get-tuple-element.42, f32[1,2,256,256]{3,2,1,0:T(8,128)S(1)} %get-tuple-element.41), kind=kOutput, calls=%fused_computation.63 | convolution fusion | flops 6442713088 | bytes 17825792 | tf_op jit(solution)/shard_map/ocqm,cnujm->onujq/dot_general | solution.py:199
  440.6 2.0 multiply_subtract_fusion.2
  442.6 3.9 fusion.28
  446.5 9.7 %copy.194 = f32[32,2,2,64,256]{4,2,3,1,0:T(2,128)} copy(f32[32,2,2,64,256]{4,0,2,3,1:T(8,128)S(1)} %fusion.28) | data formatting | bytes 16777216 | tf_op jit(solution)/shard_map/ocpn,cnujq->puojq/transpose | solution.py:201
  456.2 7.2 all-to-all-start.2
  464.1 1.4 collective-permute-start
  466.4 2.6 collective-permute-start.2
  469.2 2.0 copy.206
  471.2 2.0 copy.204
  478.1 3.3 convolution_select_fusion.1
  481.4 4.6 select_reduce_fusion
  486.0 1.8 subtract_bitcast_fusion.1
  487.9 1.3 copy.208
  489.2 1.8 reshape.1135
  493.4 150.5 %all-to-all-done.2 = f32[32,2,2,64,256]{4,2,3,1,0:T(2,128)} async-done(((f32[32,2,2,64,256]{4,2,3,1,0:T(2,128)}), f32[32,2,2,64,256]{4,2,3,1,0:T(2,128)}, u32[]{:S(2)}, u32[]{:S(2)}) %all-to-all-start.2) | async-done | bytes 8388640 | tf_op jit(solution)/shard_map/all_to_all | solution.py:202
  643.9 9.9 %all-to-all-start.4 = ((f32[16,2,2,2,572]{4,3,2,1,0:T(2,128)}), f32[16,2,2,2,572]{4,3,2,1,0:T(2,128)S(1)}, u32[]{:S(2)}, u32[]{:S(2)}) async-start(f32[16,2,2,2,572]{4,3,2,1,0:T(2,128)} %copy-done.9), calls=%async_computation.4 | async-start | bytes 655360 | tf_op jit(solution)/shard_map/all_to_all | solution.py:188
  653.8 4.7 copy.195
  658.4 3.9 convolution_bitcast_fusion
  662.3 4.9 copy.285
  667.2 1.6 multiply_subtract_fusion.1
  668.8 4.5 fusion.31
  674.5 2.4 copy.198
  676.9 2.4 copy.199
  679.4 3.6 fusion.17
  683.0 1.9 copy-done
  684.9 1.4 copy-done.2
  686.3 4.0 maximum_bitcast_fusion.5
  691.1 7.0 all-to-all-start.3
  698.1 4.8 select_reduce_fusion.1
  704.3 94.8 %all-gather = f32[32,2,2,2,572]{4,3,2,1,0:T(2,128)S(1)} all-gather(f32[16,2,2,2,572]{4,3,2,1,0:T(2,128)} %copy-done.7), channel_id=2, replica_groups=mesh['ha'=2,'az'=16] {'ha'}, dimensions={0}, use_global_device_ids=true | all-gather | bytes 878592 | tf_op jit(solution)/shard_map/all_gather | solution.py:189
  800.9 1.9 squeeze.38
  802.9 1.9 copy.211
  804.8 1.9 squeeze.39
  806.8 2.0 fusion.52
  811.0 1.4 multiply_bitcast_fusion.1
  813.3 7.6 all_gather.19
  821.0 2.9 collective-permute-start.4
  824.0 1.9 collective-permute-done.4
  825.9 3.3 collective-permute-done.5
  833.8 8.7 %copy.202 = f32[2,2,2048,256]{2,3,0,1:T(8,128)} copy(f32[2,2,2048,256]{3,2,1,0:T(8,128)} %all-to-all-done.3) | data formatting | bytes 16777216 | tf_op jit(solution)/shard_map/all_to_all | solution.py:226
  842.5 8.7 %copy.215 = f32[2,2048,512]{2,1,0:T(8,128)} copy(f32[2,2048,512]{1,2,0:T(8,128)} %bitcast.397) | data formatting | bytes 16777216
  (145 shorter events, 32.9 us)
Async XLA Ops:
  28.9 98.7 %all-to-all-start = ((f32[2,2,2048,256]{2,3,1,0:T(8,128)}), f32[2,2,2048,256]{2,3,1,0:T(8,128)}, u32[]{:S(2)}, u32[]{:S(2)}) async-start(f32[2,2,2048,256]{2,3,1,0:T(8,128)} %copy.176), calls=%async_computation | async-start | bytes 16777216 | tf_op jit(solution)/shard_map/all_to_all | solution.py:141
  167.5 6.3 copy-start.16
  167.5 199.4 %copy-start.17 = (s32[512]{0:T(512)S(1)}, s32[512]{0:T(512)}, u32[]{:S(2)}) copy-start(s32[512]{0:T(512)} %param.10) | copy-start | bytes 6148
  167.5 216.3 %copy-start.10 = (f32[16,4096]{1,0:T(8,128)S(1)}, f32[16,4096]{1,0:T(8,128)}, u32[]{:S(2)}) copy-start(f32[16,4096]{1,0:T(8,128)} %param.11) | copy-start | bytes 786436
  167.5 229.6 %all-to-all-start.1 = ((f32[32,2,2,64,256]{4,2,3,1,0:T(2,128)}), f32[32,2,2,64,256]{4,2,3,1,0:T(2,128)}, u32[]{:S(2)}, u32[]{:S(2)}) async-start(f32[32,2,2,64,256]{4,2,3,1,0:T(2,128)} %copy.180), calls=%async_computation.1 | async-start | bytes 16777216 | tf_op jit(solution)/shard_map/all_to_all | solution.py:148
  413.1 11.6 %copy-start.5 = (f32[32,256,2,64]{1,3,2,0:T(8,128)S(1)}, f32[32,256,2,64]{1,3,2,0:T(8,128)}, u32[]{:S(2)}) copy-start(f32[32,256,2,64]{1,3,2,0:T(8,128)} %fusion.44) | copy-start | bytes 12582916
  424.7 3.4 copy-start.4
  456.2 7.2 copy-start.11
  456.2 9.4 %copy-start.8 = (f32[2,128,512]{2,1,0:T(8,128)S(1)}, f32[2,128,512]{2,1,0:T(8,128)}, u32[]{:S(2)}) copy-start(f32[2,128,512]{2,1,0:T(8,128)} %param.15) | copy-start | bytes 1572868
  456.2 187.7 %all-to-all-start.2 = ((f32[32,2,2,64,256]{4,2,3,1,0:T(2,128)}), f32[32,2,2,64,256]{4,2,3,1,0:T(2,128)}, u32[]{:S(2)}, u32[]{:S(2)}) async-start(f32[32,2,2,64,256]{4,2,3,1,0:T(2,128)} %copy.194), calls=%async_computation.2 | async-start | bytes 16777216 | tf_op jit(solution)/shard_map/all_to_all | solution.py:202
  464.1 342.6 %collective-permute-start = (f32[128,30]{1,0:T(8,128)}, f32[128,30]{1,0:T(8,128)S(1)}, u32[]{:S(2)}, u32[]{:S(2)}) collective-permute-start(f32[128,30]{1,0:T(8,128)} %get-tuple-element.39), channel_id=1, source_target_pairs={{0,1},{1,2},{2,3},{3,4},{4,5},{5,6},{6,7},{7,8},{8,9},{9,10},{10,1... | collective-permute-start | bytes 46088 | tf_op jit(solution)/shard_map/ppermute | solution.py:71
  465.6 341.2 %collective-permute-start.1 = (f32[128,30]{1,0:T(8,128)}, f32[128,30]{1,0:T(8,128)S(1)}, u32[]{:S(2)}, u32[]{:S(2)}) collective-permute-start(f32[128,30]{1,0:T(8,128)} %get-tuple-element.40), channel_id=1, source_target_pairs={{1,0},{2,1},{3,2},{4,3},{5,4},{6,5},{7,6},{8,7},{9,8},{10,9},{11,1... | collective-permute-start | bytes 46088 | tf_op jit(solution)/shard_map/ppermute | solution.py:72
  466.4 237.0 %collective-permute-start.2 = (f32[2,128,15]{1,2,0:T(8,128)}, f32[2,128,15]{1,2,0:T(8,128)S(1)}, u32[]{:S(2)}, u32[]{:S(2)}) collective-permute-start(f32[2,128,15]{1,2,0:T(8,128)} %get-tuple-element.33), channel_id=1, source_target_pairs={{0,1},{1,2},{2,3},{3,4},{4,5},{5,6},{6,7},{7,8},{8,9},{9,10},{10,1... | collective-permute-start | bytes 46088 | tf_op jit(solution)/shard_map/ppermute | solution.py:71
  469.0 234.4 %collective-permute-start.3 = (f32[2,128,15]{1,2,0:T(8,128)}, f32[2,128,15]{1,2,0:T(8,128)S(1)}, u32[]{:S(2)}, u32[]{:S(2)}) collective-permute-start(f32[2,128,15]{1,2,0:T(8,128)} %get-tuple-element.34), channel_id=1, source_target_pairs={{1,0},{2,1},{3,2},{4,3},{5,4},{6,5},{7,6},{8,7},{9,8},{10,9},{11,1... | collective-permute-start | bytes 46088 | tf_op jit(solution)/shard_map/ppermute | solution.py:72
  473.2 8.1 copy-start.12
  473.3 8.1 copy-start.14
  475.7 5.7 copy-start.20
  492.6 0.7 copy-start.9
  643.9 46.5 %all-to-all-start.4 = ((f32[16,2,2,2,572]{4,3,2,1,0:T(2,128)}), f32[16,2,2,2,572]{4,3,2,1,0:T(2,128)S(1)}, u32[]{:S(2)}, u32[]{:S(2)}) async-start(f32[16,2,2,2,572]{4,3,2,1,0:T(2,128)} %copy-done.9), calls=%async_computation.4 | async-start | bytes 655360 | tf_op jit(solution)/shard_map/all_to_all | solution.py:188
  676.9 2.5 copy-start.3
  676.9 2.5 copy-start.13
  676.9 2.5 copy-start.15
  676.9 2.5 copy-start.18
  676.9 2.5 copy-start.19
  683.0 1.9 copy-start
  683.0 3.3 copy-start.2
  690.4 7.7 copy-start.21
  690.4 12.6 %copy-start.22 = (f32[63]{0:T(128)S(1)}, f32[63]{0:T(128)}, u32[]{:S(2)}) copy-start(f32[63]{0:T(128)} %param.13) | copy-start | bytes 760
  690.4 0.7 copy-start.7
  691.1 142.7 %all-to-all-start.3 = ((f32[2,2,2048,256]{3,2,1,0:T(8,128)}), f32[2,2,2048,256]{3,2,1,0:T(8,128)}, u32[]{:S(2)}, u32[]{:S(2)}) async-start(f32[2,2,2048,256]{3,2,1,0:T(8,128)} %maximum_bitcast_fusion.5), calls=%async_computation.3 | async-start | bytes 16777216 | tf_op jit(solution)/shard_map/all_to_all | solution.py:226
  799.1 11.0 %copy-start.6 = (f32[2,128,542]{1,2,0:T(8,128)S(1)}, f32[2,128,542]{1,2,0:T(8,128)}, u32[]{:S(2)}) copy-start(f32[2,128,542]{1,2,0:T(8,128)} %pad_maximum_fusion.5) | copy-start | bytes 1665028
  806.7 5.6 copy-start.1
  821.0 4.8 collective-permute-start.4
  823.9 5.3 collective-permute-start.5

commit v2 on v1

--- a/solution.py
+++ b/solution.py
@@ -73,6 +73,29 @@
     return left, right
 
 
+def choose(options, index):
+    picked = options[0]
+    for i in range(1, len(options)):
+        picked = jnp.where(index == i, options[i], picked)
+    return picked
+
+
+def ha_trade(piece_for):
+    count = lax.axis_size("ha")
+    slab = lax.axis_index("ha")
+    parts = [piece_for(slab)]
+    for shift in range(1, count):
+        pairs = [(i, (i + shift) % count) for i in range(count)]
+        parts.append(lax.ppermute(piece_for((slab + shift) % count), "ha", pairs))
+    return parts
+
+
+def ha_order(parts):
+    count = len(parts)
+    slab = lax.axis_index("ha")
+    return [choose(parts, (slab - source) % count) for source in range(count)]
+
+
 def local(field, terrain, profile_pick, profile_table, clutter_mask, pulse, beam, measured):
     n_ha = lax.axis_size("ha")
     n_az = lax.axis_size("az")
@@ -80,6 +103,8 @@
     slab = lax.axis_index("ha")
     block = lax.axis_index("az")
     place = block * n_ha + slab
+    gathered = lax.all_gather(jnp.stack([profile_pick, terrain]), "az", axis=1, tiled=True)
+    field, gathered = lax.optimization_barrier((field, gathered))
     both = ("az", "ha")
     h_dev, a_dev = field.shape[1], field.shape[2]
     total_h, total_a = h_dev * n_ha, a_dev * n_az
@@ -88,6 +113,8 @@
     h_first = max(64, n_dev)
     h_second = total_h // h_first
     own = h_first // n_dev
+    lanes = 128 if cols % 128 == 0 else cols
+    chunks = cols // lanes
     n_prof = profile_table.shape[0]
 
     taps_range = pulse.shape[0]
@@ -107,7 +134,11 @@
     left, right = halo(measured, half_beam)
     wide_measured = jnp.concatenate([left, measured, right], axis=2)
 
-    def sources_of(low_re, low_im, step):
+    def sources_of(strip, step):
+        strip = jnp.concatenate(ha_order(ha_trade(lambda to: strip)), axis=2)
+        left, right = halo(strip, reach)
+        strip = jnp.concatenate([left, strip, right], axis=2)
+        low_re, low_im = strip[0], strip[1]
         power = wide_mask * (low_re * low_re + low_im * low_im)
         ranged = jnp.dot(rmat, power, precision=EXACT)
         misfit = jnp.dot(ranged, forward_band, precision=EXACT) - wide_measured[step]
@@ -119,8 +150,7 @@
         ]
         return jnp.stack([weight * mine[0], weight * mine[1]])
 
-    all_pick = lax.all_gather(profile_pick, "az", tiled=True)
-    all_terrain = lax.all_gather(terrain, "az", tiled=True)
+    all_pick, all_terrain = gathered[0], gathered[1]
     height = iota((1, total_h), 1)
     z_chirp = chirp(height, height_chirp, total_h)
     z_gain = gauss(height_chirp, total_h)
@@ -129,30 +159,47 @@
     amount = damping(height, total_h)
     bend = cmul((amount * jnp.cos(profile_table), amount * jnp.sin(profile_table)), cmul(z_chirp, gain))
     bend_again = cmul(bend, z_chirp)
-
     slab_z = chirp(slab * h_dev + iota((h_dev, 1), 0), height_chirp, total_h)
     block_y = chirp(block * a_dev + iota((1, a_dev), 1), azimuth_chirp, total_a)
-    start = cmul((field[0], field[1]), cmul(slab_z, block_y))
-    start = jnp.stack(start).reshape(2, h_dev, n_ha, cols).transpose(2, 0, 1, 3)
-
     w_first = roots(h_first, height_chirp, total_h)
     w_second = roots(h_second, height_chirp, total_h)
+    w_in = w_first.reshape(2, 2, h_first, n_ha, h_first // n_ha)
     tw_re, tw_im = (t[:, :, None] for t in twist(h_first, h_second, height_chirp, total_h))
-    tall = lax.all_to_all(start, "ha", split_axis=0, concat_axis=0)
-    tall = tall.reshape(n_ha, 2, h_first // n_ha, h_second, cols)
-    w_in = w_first.reshape(2, 2, h_first, n_ha, h_first // n_ha)
-    tall = jnp.einsum("ocksa,scabq->okbq", w_in, tall, precision=FAST)
-    tall = jnp.stack(cmul(tall, (tw_re, tw_im)))
-    tall = jnp.einsum("ocjb,ckbq->kojq", w_second, tall, precision=FAST)
-    tall = tall.reshape(n_dev, own, 2, h_second, cols)
-    rows = lax.all_to_all(tall, both, split_axis=0, concat_axis=0)
-
     w_blocks = roots(n_dev, azimuth_chirp, total_a)
     w_cols = roots(cols, azimuth_chirp, total_a)
     ty_re, ty_im = (t[:, None, None, :] for t in twist(n_dev, cols, azimuth_chirp, total_a))
-    rows = jnp.einsum("ocnp,pucjq->onujq", w_blocks, rows, precision=FAST)
-    rows = jnp.stack(cmul(rows, (ty_re, ty_im)))
-    rows = jnp.einsum("ocmq,cnujq->onujm", w_cols, rows, precision=FAST)
+
+    def send_chunk(chunk):
+        def piece_for(to):
+            def columns(cells):
+                return choose(
+                    [cells[..., i * cols + chunk * lanes:][..., :lanes] for i in range(n_ha)], to
+                )
+
+            y_part = (columns(block_y[0]), columns(block_y[1]))
+            return jnp.stack(cmul((columns(field[0]), columns(field[1])), cmul(slab_z, y_part)))
+
+        return ha_trade(piece_for)
+
+    def to_rows(parts):
+        tall = 0.0
+        for shift, part in enumerate(parts):
+            part = part.reshape(2, h_first // n_ha, h_second, lanes)
+            w_part = lax.dynamic_index_in_dim(w_in, (slab - shift) % n_ha, 3, False)
+            tall = tall + jnp.einsum("ocka,cabq->okbq", w_part, part, precision=FAST)
+        tall = jnp.stack(cmul(tall, (tw_re, tw_im)))
+        tall = jnp.einsum("ocjb,ckbq->kojq", w_second, tall, precision=FAST)
+        tall = tall.reshape(n_dev, own, 2, h_second, lanes)
+        return lax.all_to_all(tall, both, split_axis=0, concat_axis=0)
+
+    sent = [send_chunk(chunk) for chunk in range(chunks)]
+    arrived = [to_rows(parts) for parts in sent]
+    rows = 0.0
+    for chunk, part in enumerate(arrived):
+        span = slice(chunk * lanes, (chunk + 1) * lanes)
+        part = jnp.einsum("ocnp,pucjq->onujq", w_blocks, part, precision=FAST)
+        part = jnp.stack(cmul(part, (ty_re[..., span], ty_im[..., span])))
+        rows = rows + jnp.einsum("ocmq,cnujq->onujm", w_cols[..., span], part, precision=FAST)
 
     def own_rows(table):
         table = table.reshape(n_prof, h_second, n_dev, own)
@@ -173,6 +220,15 @@
     )
     next_rows = jnp.stack(cmul(rows, cmul(bent, y_turn)))
 
+    def to_tall(chunk):
+        span = slice(chunk * lanes, (chunk + 1) * lanes)
+        part = jnp.einsum("ocqm,cnujm->onujq", w_cols[:, :, span], next_rows, precision=FAST)
+        part = jnp.stack(cmul(part, (ty_re[..., span], ty_im[..., span])))
+        part = jnp.einsum("ocpn,cnujq->puojq", w_blocks, part, precision=FAST)
+        return lax.all_to_all(part, both, split_axis=0, concat_axis=0)
+
+    returned = [to_tall(chunk) for chunk in range(chunks)]
+
     n_low = -(-bottom // h_first)
     low_bend = tuple(
         ground[:, :, :n_low]
@@ -181,50 +237,36 @@
     )
     low_chirp = tuple(t[:, None, None, :] for t in y_chirp)
     low = jnp.stack(cmul(rows[:, :, :, :n_low], cmul(low_bend, low_chirp)))
-    low = low.transpose(0, 2, 3, 4, 1).reshape(2, own, n_low, total_a)
-    low = jnp.concatenate([low[..., total_a - reach:], low, low[..., :reach]], axis=-1)
-    if bottom % h_first == 0:
-        windows = jnp.stack([low[..., i * a_dev:i * a_dev + wide] for i in range(n_az)])
-        windows = lax.all_to_all(windows, "az", split_axis=0, concat_axis=0)
-        windows = lax.all_gather(windows, "ha")
-        windows = windows.transpose(2, 4, 1, 0, 3, 5).reshape(2, bottom, wide)
-    else:
-        spread = jnp.zeros((2, h_first, n_low, low.shape[-1]), jnp.float32)
-        spread = lax.dynamic_update_slice_in_dim(spread, low, place * own, 1)
-        spread = jnp.swapaxes(spread, 1, 2).reshape(2, n_low * h_first, low.shape[-1])
-        spread = lax.psum(spread[:, :bottom], both)
-        windows = lax.dynamic_slice_in_dim(spread, block * a_dev, wide, 2)
-    first_sources = sources_of(windows[0], windows[1], 0)
-
-    rows = jnp.einsum("ocqm,cnujm->onujq", w_cols, next_rows, precision=FAST)
-    rows = jnp.stack(cmul(rows, (ty_re, ty_im)))
-    rows = jnp.einsum("ocpn,cnujq->puojq", w_blocks, rows, precision=FAST)
-    tall = lax.all_to_all(rows, both, split_axis=0, concat_axis=0)
-    tall = tall.reshape(h_first, 2, h_second, cols)
-    tall = jnp.einsum("ocbj,kcjq->okbq", w_second, tall, precision=FAST)
-    tall = jnp.stack(cmul(tall, (tw_re, tw_im)))
-    tall = jnp.einsum("ocak,ckbq->oabq", w_first, tall, precision=FAST)
-    tall = tall.reshape(2, total_h, cols)
-
-    col_start = slab * cols
-    tall_pick = lax.dynamic_slice_in_dim(profile_pick, col_start, cols, 0)
-    tall_terrain = lax.dynamic_slice_in_dim(terrain, col_start, cols, 0)
-    tall_hot = onehot_of(tall_pick, n_prof)
-    tall_ground = (iota((total_h, 1), 0) >= tall_terrain[None, :]).astype(jnp.float32)
-    tall_y = chirp(block * a_dev + col_start + iota((1, cols), 1), azimuth_chirp, total_a)
-    tall_bent = tuple(
-        tall_ground * jnp.einsum("fh,fq->hq", t, tall_hot, precision=FAST) for t in bend
-    )
-    last = jnp.stack(cmul(tall, cmul(tall_bent, tall_y)))
-
-    strip = lax.all_gather(last[:, :bottom], "ha", axis=2, tiled=True)
-    left, right = halo(strip, reach)
-    strip = jnp.concatenate([left, strip, right], axis=2)
-    second_sources = sources_of(strip[0], strip[1], 1)
-
-    out = last.reshape(2, n_ha, h_dev, cols).transpose(1, 0, 2, 3)
-    out = lax.all_to_all(out, "ha", split_axis=0, concat_axis=0)
-    out = out.transpose(1, 2, 0, 3).reshape(2, h_dev, a_dev)
+    low = low.transpose(0, 2, 3, 4, 1).reshape(2, own, n_low, n_dev, cols)
+    low = lax.all_to_all(low.transpose(3, 0, 1, 2, 4), both, split_axis=0, concat_axis=0)
+    low = low.transpose(1, 3, 0, 2, 4).reshape(2, n_low * h_first, cols)[:, :bottom]
+    first_sources = sources_of(low, 0)
+
+    lasts = []
+    outs = []
+    for chunk, part in enumerate(returned):
+        part = part.reshape(h_first, 2, h_second, lanes)
+        part = jnp.einsum("ocbj,kcjq->okbq", w_second, part, precision=FAST)
+        part = jnp.stack(cmul(part, (tw_re, tw_im)))
+        part = jnp.einsum("ocak,ckbq->oabq", w_first, part, precision=FAST)
+        part = part.reshape(2, total_h, lanes)
+        col_start = slab * cols + chunk * lanes
+        tall_pick = lax.dynamic_slice_in_dim(profile_pick, col_start, lanes, 0)
+        tall_terrain = lax.dynamic_slice_in_dim(terrain, col_start, lanes, 0)
+        tall_hot = onehot_of(tall_pick, n_prof)
+        tall_ground = (iota((total_h, 1), 0) >= tall_terrain[None, :]).astype(jnp.float32)
+        tall_y = chirp(block * a_dev + col_start + iota((1, lanes), 1), azimuth_chirp, total_a)
+        tall_bent = tuple(
+            tall_ground * jnp.einsum("fh,fq->hq", t, tall_hot, precision=FAST) for t in bend
+        )
+        last = jnp.stack(cmul(part, cmul(tall_bent, tall_y)))
+        lasts.append(last)
+        outs.append(
+            ha_order(ha_trade(lambda to: lax.dynamic_slice_in_dim(last, to * h_dev, h_dev, 1)))
+        )
+    strip = jnp.concatenate([last[:, :bottom] for last in lasts], axis=2)
+    second_sources = sources_of(strip, 1)
+    out = jnp.concatenate([outs[j][i] for i in range(n_ha) for j in range(chunks)], axis=2)
     return (out, jnp.stack([first_sources, second_sources]))
 
 

time: 862 us -> 765 us (0.89)
  blocking collectives: 312 us -> 15.8 us
  waiting for transfers between devices: 247 us -> 435 us
  matrix products: 92.7 us -> 112 us
  local copies, waits for them, and re-layouts: 112 us -> 93 us
  other arithmetic: 42.3 us -> 54 us
    all_gather x4 -> x1, blocking collectives: 312 us -> 15.8 us  [local(): lax.all_gather(jnp.stack([profile_pick, terrain]), 'az', axis=1, tiled=True)]
    ppermute x0 -> x6, waiting for transfers between devices: none -> 166 us  [ha_trade(): parts.append(lax.ppermute(piece_for((slab + shift) % count), 'ha', pairs))]
    ppermute x3 -> x4, waiting for transfers between devices: 3.35 us -> 60.8 us  [halo(): lax.ppermute(head, axis, [((i + 1) % count, i) for i in range(count)])]
    all_to_all x5, waiting for transfers between devices: 241 us -> 208 us  [the longest x2 138 us: to_rows(): return lax.all_to_all(tall, both, split_axis=0, concat_axis=0)]
    all_to_all x3 -> x2, local copies, waits for them, and re-layouts: 22.1 us -> 5.56 us  [to_tall(): return lax.all_to_all(part, both, split_axis=0, concat_axis=0)]
    dot_general x8 -> x18, matrix products: 68 us -> 82.5 us  [the longest x2 20.6 us: to_tall(): jnp.einsum('ocqm,cnujm->onujq', w_cols[:, :, span], next_rows, precision=...]
    unnamed x64 -> x118, local copies, waits for them, and re-layouts: 25.7 us -> 13.8 us
    slice x6 -> x5, local copies, waits for them, and re-layouts: 11.6 us -> 0.24 us  [the longest x1 0.16 us: local(): all_pick, all_terrain = (gathered[0], gathered[1])]
  transfers between devices with their start and end apart: 11 -> 19, of which waited for: 4 -> 12; matrix products, arithmetic and copies ran while one was open for 11% -> 19% of each run, Pallas kernels for 0% -> 0%
where the time goes in v2:
time: 765 us; the launch traced here: 761 us
  waiting for transfers between devices  435 us (57%)
  matrix products  112 us (15%)
  local copies, waits for them, and re-layouts  93 us (12%)
  other arithmetic  54 us (7%)
  starting transfers between devices  49.3 us (6%)
  blocking collectives  15.8 us (2%)
    ppermute x6, waiting for transfers between devices, ha_trade(): parts.append(lax.ppermute(piece_for((slab + shift) % count), 'ha', pairs))  166 us
    all_to_all x2, waiting for transfers between devices, to_rows(): return lax.all_to_all(tall, both, split_axis=0, concat_axis=0)  138 us
    all_to_all x2, waiting for transfers between devices, to_tall(): return lax.all_to_all(part, both, split_axis=0, concat_axis=0)  69.8 us
    ppermute x4, waiting for transfers between devices, halo(): lax.ppermute(head, axis, [((i + 1) % count, i) for i in range(count)])  60.8 us
    dot_general x2, matrix products, to_tall(): jnp.einsum('ocqm,cnujm->onujq', w_cols[:, :, span], next_rows, precision=...  20.6 us
    all_to_all x2, starting transfers between devices, to_rows(): return lax.all_to_all(tall, both, split_axis=0, concat_axis=0)  18.9 us
    all_gather x1, blocking collectives, local(): lax.all_gather(jnp.stack([profile_pick, terrain]), 'az', axis=1, tiled=True)  15.8 us
  transfers between devices with their start and end apart: 19, of which 12 were waited for; matrix products, arithmetic and copies ran while one was open for 19% of the time, Pallas kernels for 0%

profile of v2, /device:TPU:11, one launch (start us, length us, event | category | flops | bytes accessed | tf_op | source)
XLA Modules:
  0.0 761.5 jit_solution(6363537172834235686)
XLA Ops:
  1.6 15.8 %all_gather.3 = s32[2,8192]{1,0:T(2,128)S(1)} all-gather(s32[2,512]{1,0:T(2,128)S(1)} %pad_add_fusion), channel_id=1, replica_groups=mesh['ha'=2,'az'=16] {'az'}, dimensions={1}, use_global_device_ids=true | all-gather | bytes 69632 | tf_op jit(solution)/shard_map/all_gather | solution.py:106
  17.4 4.4 slice_bitcast_fusion.2
  28.4 2.0 multiply_subtract_fusion.15
  38.6 32.8 %collective-permute-done.1 = f32[2,2048,128]{2,1,0:T(8,128)} collective-permute-done((f32[2,2048,128]{2,1,0:T(8,128)}, f32[2,2048,128]{2,1,0:T(8,128)}, u32[]{:S(2)}, u32[]{:S(2)}) %collective-permute-start.1) | collective-permute-done | bytes 2097184 | tf_op jit(solution)/shard_map/ppermute | solution.py:89
  71.4 4.5 bitcast_add_fusion.1
  76.0 40.4 %collective-permute-done = f32[2,2048,128]{2,1,0:T(8,128)} collective-permute-done((f32[2,2048,128]{2,1,0:T(8,128)}, f32[2,2048,128]{2,1,0:T(8,128)}, u32[]{:S(2)}, u32[]{:S(2)}) %collective-permute-start) | collective-permute-done | bytes 2097184 | tf_op jit(solution)/shard_map/ppermute | solution.py:89
  116.4 4.8 bitcast_add_fusion.2
  121.2 2.9 multiply_subtract_fusion.10
  124.6 4.2 fusion.23
  128.8 5.9 copy.170
  134.7 11.3 %all-to-all-start = ((f32[32,2,2,64,128]{4,2,3,1,0:T(2,128)}), f32[32,2,2,64,128]{4,2,3,1,0:T(2,128)}, u32[]{:S(2)}, u32[]{:S(2)}) async-start(f32[32,2,2,64,128]{4,2,3,1,0:T(2,128)} %copy.170), calls=%async_computation | async-start | bytes 8388608 | tf_op jit(solution)/shard_map/all_to_all | solution.py:193
  146.0 2.0 maximum_bitcast_fusion.3
  148.0 4.2 fusion.17
  152.3 5.8 copy.177
  158.1 78.3 %all-to-all-done = f32[32,2,2,64,128]{4,2,3,1,0:T(2,128)} async-done(((f32[32,2,2,64,128]{4,2,3,1,0:T(2,128)}), f32[32,2,2,64,128]{4,2,3,1,0:T(2,128)}, u32[]{:S(2)}, u32[]{:S(2)}) %all-to-all-start) | async-done | bytes 4194336 | tf_op jit(solution)/shard_map/all_to_all | solution.py:193
  236.4 7.5 all-to-all-start.1
  248.8 1.9 copy.216
  261.5 3.4 fusion.86
  264.9 6.4 fusion.31
  272.2 2.7 maximum_bitcast_fusion.2
  274.9 59.7 %all-to-all-done.1 = f32[32,2,2,64,128]{4,2,3,1,0:T(2,128)} async-done(((f32[32,2,2,64,128]{4,2,3,1,0:T(2,128)}), f32[32,2,2,64,128]{4,2,3,1,0:T(2,128)}, u32[]{:S(2)}, u32[]{:S(2)}) %all-to-all-start.1) | async-done | bytes 4194336 | tf_op jit(solution)/shard_map/all_to_all | solution.py:193
  334.6 6.4 fusion.34
  342.1 6.7 fusion.13
  348.8 7.1 fusion
  355.9 3.4 copy-done.9
  361.7 7.2 all-to-all-start.4
  368.9 6.7 subtract_bitcast_fusion
  376.7 7.8 %fusion.52 = f32[2,32,2,64,128]{4,1,3,2,0:T(8,128)S(1)} fusion(f32[2,32,2,64,256,1]{4,3,2,1,0,5:T(8,128)S(1)} %maximum_bitcast_fusion, f32[1,2,256,256]{3,2,1,0:T(8,128)S(1)} %get-tuple-element.77, f32[1,2,256,256]{3,2,1,0:T(8,128)S(1)} %get-tuple-element.78), kind=kOutput, calls=%fused_computation.81 | convolution fusion | flops 3221356544 | bytes 13631488 | tf_op jit(solution)/shard_map/ocqm,cnujm->onujq/dot_general | solution.py:225
  385.1 2.0 fusion.43
  387.1 5.7 copy.204
  392.7 5.9 all-to-all-start.3
  398.6 12.8 %fusion.49 = f32[2,32,2,64,128]{4,1,3,2,0:T(8,128)S(1)} fusion(f32[2,32,2,64,256,1]{4,3,2,1,0,5:T(8,128)} %copy-done, f32[1,2,256,256]{3,2,1,0:T(8,128)S(1)} %get-tuple-element.78, f32[1,2,256,256]{3,2,1,0:T(8,128)S(1)} %get-tuple-element.77), kind=kOutput, calls=%fused_computation.80 | convolution fusion | flops 3221356544 | bytes 13631488 | tf_op jit(solution)/shard_map/ocqm,cnujm->onujq/dot_general | solution.py:225
  412.3 2.0 fusion.37
  414.3 5.2 copy.191
  419.5 69.8 %all-to-all-done.3 = f32[32,2,2,64,128]{4,2,3,1,0:T(2,128)} async-done(((f32[32,2,2,64,128]{4,2,3,1,0:T(2,128)}), f32[32,2,2,64,128]{4,2,3,1,0:T(2,128)}, u32[]{:S(2)}, u32[]{:S(2)}) %all-to-all-start.3) | async-done | bytes 4194336 | tf_op jit(solution)/shard_map/all_to_all | solution.py:228
  489.3 7.3 all-to-all-start.2
  500.5 2.1 collective-permute-start.9
  504.8 2.2 convolution_select_fusion.2
  507.0 3.4 select_reduce_fusion.1
  510.5 4.6 select_reduce_fusion
  518.3 2.1 convolution_select_fusion
  520.4 14.1 %collective-permute-done.6 = f32[2,128,256]{1,2,0:T(8,128)S(1)} collective-permute-done((f32[2,128,256]{1,2,0:T(8,128)S(1)}, f32[2,128,256]{1,2,0:T(8,128)S(1)}, u32[]{:S(2)}, u32[]{:S(2)}) %collective-permute-start.6) | collective-permute-done | bytes 262176 | tf_op jit(solution)/shard_map/ppermute | solution.py:89
  534.7 55.1 %collective-permute-done.10 = f32[2,128,15]{1,2,0:T(8,128)} collective-permute-done((f32[2,128,15]{1,2,0:T(8,128)}, f32[2,128,15]{1,2,0:T(8,128)}, u32[]{:S(2)}, u32[]{:S(2)}) %collective-permute-start.10) | collective-permute-done | bytes 15392 | tf_op jit(solution)/shard_map/ppermute | solution.py:72
  590.8 3.4 collective-permute-done.8
  598.6 2.8 copy.205
  603.3 4.5 copy.356
  607.7 2.8 copy.192
  612.4 2.8 copy.357
  615.3 3.4 multiply_subtract_fusion.5
  618.7 2.0 fusion.40
  623.6 1.9 copy.196
  625.6 2.8 copy.197
  630.2 4.2 fusion.46
  639.3 2.8 copy.210
  642.1 2.0 copy.211
  644.2 4.9 add_bitcast_fusion.2
  654.2 5.4 collective-permute-done.11
  662.6 2.2 collective-permute-done.13
  669.6 35.0 %collective-permute-done.2 = f32[2,2048,128]{1,2,0:T(8,128)} collective-permute-done((f32[2,2048,128]{1,2,0:T(8,128)}, f32[2,2048,128]{1,2,0:T(8,128)}, u32[]{:S(2)}, u32[]{:S(2)}) %collective-permute-start.2) | collective-permute-done | bytes 2097184 | tf_op jit(solution)/shard_map/ppermute | solution.py:89
  704.6 3.6 broadcast_select_fusion.3
  708.2 38.4 %collective-permute-done.3 = f32[2,2048,128]{1,2,0:T(8,128)} collective-permute-done((f32[2,2048,128]{1,2,0:T(8,128)}, f32[2,2048,128]{1,2,0:T(8,128)}, u32[]{:S(2)}, u32[]{:S(2)}) %collective-permute-start.3) | collective-permute-done | bytes 2097184 | tf_op jit(solution)/shard_map/ppermute | solution.py:89
  746.6 2.1 broadcast_select_fusion.2
  748.7 3.9 pad_maximum_fusion
  752.6 8.7 %copy.231 = f32[2,2048,512]{2,1,0:T(8,128)} copy(f32[2,2048,512]{1,2,0:T(8,128)} %pad_maximum_fusion) | data formatting | bytes 16777216
  (254 shorter events, 78.9 us)
Async XLA Ops:
  24.0 47.4 %collective-permute-start.1 = (f32[2,2048,128]{2,1,0:T(8,128)}, f32[2,2048,128]{2,1,0:T(8,128)}, u32[]{:S(2)}, u32[]{:S(2)}) collective-permute-start(f32[2,2048,128]{2,1,0:T(8,128)} %pad_maximum_fusion.4), channel_id=1, source_target_pairs={{0,16},{16,0},{1,17},{17,1},{2,18},{18,2},{3,19},{19,3},{4,20},{20... | collective-permute-start | bytes 6291464 | tf_op jit(solution)/shard_map/ppermute | solution.py:89
  27.5 88.9 %collective-permute-start = (f32[2,2048,128]{2,1,0:T(8,128)}, f32[2,2048,128]{2,1,0:T(8,128)}, u32[]{:S(2)}, u32[]{:S(2)}) collective-permute-start(f32[2,2048,128]{2,1,0:T(8,128)} %pad_maximum_fusion.3), channel_id=1, source_target_pairs={{0,16},{16,0},{1,17},{17,1},{2,18},{18,2},{3,19},{19,3},{4,20},{20... | collective-permute-start | bytes 6291464 | tf_op jit(solution)/shard_map/ppermute | solution.py:89
  34.3 86.9 %copy-start.31 = (f32[64,64]{0,1:T(8,128)}, f32[64,64]{0,1:T(8,128)S(1)}, u32[]{:S(2)}) copy-start(f32[64,64]{0,1:T(8,128)S(1)} %get-tuple-element.120) | copy-start | bytes 49156
  34.3 86.9 %copy-start.33 = (f32[64,64]{0,1:T(8,128)}, f32[64,64]{0,1:T(8,128)S(1)}, u32[]{:S(2)}) copy-start(f32[64,64]{0,1:T(8,128)S(1)} %get-tuple-element.121) | copy-start | bytes 49156
  34.8 113.3 %copy-start.20 = (f32[1,2,64,64]{3,2,1,0:T(8,128)}, f32[1,2,64,64]{3,2,1,0:T(8,128)S(1)}, u32[]{:S(2)}) copy-start(f32[1,2,64,64]{3,2,1,0:T(8,128)S(1)} %get-tuple-element.88) | copy-start | bytes 98308
  134.7 101.7 %all-to-all-start = ((f32[32,2,2,64,128]{4,2,3,1,0:T(2,128)}), f32[32,2,2,64,128]{4,2,3,1,0:T(2,128)}, u32[]{:S(2)}, u32[]{:S(2)}) async-start(f32[32,2,2,64,128]{4,2,3,1,0:T(2,128)} %copy.170), calls=%async_computation | async-start | bytes 8388608 | tf_op jit(solution)/shard_map/all_to_all | solution.py:193
  158.1 86.1 %copy-start.35 = (f32[16,4096]{1,0:T(8,128)S(1)}, f32[16,4096]{1,0:T(8,128)}, u32[]{:S(2)}) copy-start(f32[16,4096]{1,0:T(8,128)} %param.11) | copy-start | bytes 786436
  236.4 98.2 %all-to-all-start.1 = ((f32[32,2,2,64,128]{4,2,3,1,0:T(2,128)}), f32[32,2,2,64,128]{4,2,3,1,0:T(2,128)}, u32[]{:S(2)}, u32[]{:S(2)}) async-start(f32[32,2,2,64,128]{4,2,3,1,0:T(2,128)} %copy.177), calls=%async_computation.1 | async-start | bytes 8388608 | tf_op jit(solution)/shard_map/all_to_all | solution.py:193
  245.5 6.1 copy-start.15
  342.1 6.7 copy-start.5
  355.9 3.4 copy-start.9
  361.7 31.1 %all-to-all-start.4 = ((f32[32,2,2,2,256]{4,3,2,1,0:T(2,128)}), f32[32,2,2,2,256]{4,3,2,1,0:T(2,128)S(1)}, u32[]{:S(2)}, u32[]{:S(2)}) async-start(f32[32,2,2,2,256]{4,3,2,1,0:T(2,128)} %copy.221), calls=%async_computation.4 | async-start | bytes 524288 | tf_op jit(solution)/shard_map/all_to_all | solution.py:241
  376.7 7.8 %copy-start = (f32[2,32,2,64,256,1]{4,3,2,1,0,5:T(8,128)}, f32[2,32,2,64,256,1]{4,3,2,1,0,5:T(8,128)S(1)}, u32[]{:S(2)}) copy-start(f32[2,32,2,64,256,1]{4,3,2,1,0,5:T(8,128)S(1)} %maximum_bitcast_fusion) | copy-start | bytes 25165828
  392.7 96.6 %all-to-all-start.3 = ((f32[32,2,2,64,128]{4,2,3,1,0:T(2,128)}), f32[32,2,2,64,128]{4,2,3,1,0:T(2,128)}, u32[]{:S(2)}, u32[]{:S(2)}) async-start(f32[32,2,2,64,128]{4,2,3,1,0:T(2,128)} %copy.204), calls=%async_computation.3 | async-start | bytes 8388608 | tf_op jit(solution)/shard_map/all_to_all | solution.py:228
  419.5 77.1 %copy-start.36 = (s32[128,512]{1,0:T(8,128)S(1)}, s32[128,512]{1,0:T(8,128)}, u32[]{:S(2)}) copy-start(s32[128,512]{1,0:T(8,128)} %param.12) | copy-start | bytes 786436
  419.5 79.4 %copy-start.30 = (f32[2,128,512]{2,1,0:T(8,128)S(1)}, f32[2,128,512]{2,1,0:T(8,128)}, u32[]{:S(2)}) copy-start(f32[2,128,512]{2,1,0:T(8,128)} %param.15) | copy-start | bytes 1572868
  489.3 118.4 %all-to-all-start.2 = ((f32[32,2,2,64,128]{4,2,3,1,0:T(2,128)}), f32[32,2,2,64,128]{4,2,3,1,0:T(2,128)}, u32[]{:S(2)}, u32[]{:S(2)}) async-start(f32[32,2,2,64,128]{4,2,3,1,0:T(2,128)} %copy.191), calls=%async_computation.2 | async-start | bytes 8388608 | tf_op jit(solution)/shard_map/all_to_all | solution.py:228
  496.6 7.3 copy-start.41
  496.6 7.3 copy-start.42
  496.7 7.5 copy-start.52
  496.8 100.2 %copy-start.13 = (f32[128,512]{0,1:T(8,128)}, f32[128,512]{0,1:T(8,128)S(1)}, u32[]{:S(2)}) copy-start(f32[128,512]{0,1:T(8,128)S(1)} %convert_element_type.318) | copy-start | bytes 786436
  497.5 96.8 %collective-permute-start.4 = (f32[128,30]{0,1:T(8,128)}, f32[128,30]{0,1:T(8,128)S(1)}, u32[]{:S(2)}, u32[]{:S(2)}) collective-permute-start(f32[128,30]{0,1:T(8,128)} %get-tuple-element.75), channel_id=1, source_target_pairs={{0,1},{1,2},{2,3},{3,4},{4,5},{5,6},{6,7},{7,8},{8,9},{9,10},{10,1... | collective-permute-start | bytes 46088 | tf_op jit(solution)/shard_map/ppermute | solution.py:71
  498.9 95.4 %collective-permute-start.5 = (f32[128,30]{0,1:T(8,128)}, f32[128,30]{0,1:T(8,128)S(1)}, u32[]{:S(2)}, u32[]{:S(2)}) collective-permute-start(f32[128,30]{0,1:T(8,128)} %get-tuple-element.76), channel_id=1, source_target_pairs={{1,0},{2,1},{3,2},{4,3},{5,4},{6,5},{7,6},{8,7},{9,8},{10,9},{11,1... | collective-permute-start | bytes 46088 | tf_op jit(solution)/shard_map/ppermute | solution.py:72
  499.1 5.7 copy-start.22
  499.8 90.0 %collective-permute-start.10 = (f32[2,128,15]{1,2,0:T(8,128)}, f32[2,128,15]{1,2,0:T(8,128)}, u32[]{:S(2)}, u32[]{:S(2)}) collective-permute-start(f32[2,128,15]{1,2,0:T(8,128)} %get-tuple-element.68), channel_id=1, source_target_pairs={{1,0},{2,1},{3,2},{4,3},{5,4},{6,5},{7,6},{8,7},{9,8},{10,9},{11,1... | collective-permute-start | bytes 46088 | tf_op jit(solution)/shard_map/ppermute | solution.py:72
  500.5 89.5 %collective-permute-start.9 = (f32[2,128,15]{1,2,0:T(8,128)}, f32[2,128,15]{1,2,0:T(8,128)}, u32[]{:S(2)}, u32[]{:S(2)}) collective-permute-start(f32[2,128,15]{1,2,0:T(8,128)} %get-tuple-element.67), channel_id=1, source_target_pairs={{0,1},{1,2},{2,3},{3,4},{4,5},{5,6},{6,7},{7,8},{8,9},{9,10},{10,1... | collective-permute-start | bytes 46088 | tf_op jit(solution)/shard_map/ppermute | solution.py:71
  503.9 14.3 %copy-start.43 = (s32[128]{0:T(128)}, s32[128]{0:T(128)S(1)}, u32[]{:S(2)}) copy-start(s32[128]{0:T(128)S(1)} %get-tuple-element.92) | copy-start | bytes 1540
  504.0 14.3 %copy-start.45 = (s32[128]{0:T(128)}, s32[128]{0:T(128)S(1)}, u32[]{:S(2)}) copy-start(s32[128]{0:T(128)S(1)} %get-tuple-element.118) | copy-start | bytes 1540
  504.1 2.9 copy-start.51
  504.7 92.3 %copy-start.26 = (f32[128,128]{1,0:T(8,128)}, f32[128,128]{1,0:T(8,128)S(1)}, u32[]{:S(2)}) copy-start(f32[128,128]{1,0:T(8,128)S(1)} %select_reduce_fusion.2) | copy-start | bytes 196612
  510.5 85.6 %copy-start.7 = (f32[542,512]{1,0:T(8,128)}, f32[542,512]{1,0:T(8,128)S(1)}, u32[]{:S(2)}) copy-start(f32[542,512]{1,0:T(8,128)S(1)} %select_reduce_fusion.1) | copy-start | bytes 3330052
  517.0 73.0 %copy-start.23 = (f32[2,128,512]{1,2,0:T(8,128)S(1)}, f32[2,128,512]{1,2,0:T(8,128)}, u32[]{:S(2)}) copy-start(f32[2,128,512]{1,2,0:T(8,128)} %copy-done.22) | copy-start | bytes 1572868
  517.0 17.6 %collective-permute-start.6 = (f32[2,128,256]{1,2,0:T(8,128)S(1)}, f32[2,128,256]{1,2,0:T(8,128)S(1)}, u32[]{:S(2)}, u32[]{:S(2)}) collective-permute-start(f32[2,128,256]{1,2,0:T(8,128)S(1)} %copy.223), channel_id=1, source_target_pairs={{0,16},{16,0},{1,17},{17,1},{2,18},{18,2},{3,19},{19,3},{4,20},{20... | collective-permute-start | bytes 786440 | tf_op jit(solution)/shard_map/ppermute | solution.py:89
  534.6 56.2 %collective-permute-start.7 = (f32[2,128,30]{1,2,0:T(8,128)S(1)}, f32[2,128,30]{1,2,0:T(8,128)S(1)}, u32[]{:S(2)}, u32[]{:S(2)}) collective-permute-start(f32[2,128,30]{1,2,0:T(8,128)S(1)} %slice.446), channel_id=1, source_target_pairs={{0,1},{1,2},{2,3},{3,4},{4,5},{5,6},{6,7},{7,8},{8,9},{9,10},{10,1... | collective-permute-start | bytes 92168 | tf_op jit(solution)/shard_map/ppermute | solution.py:71
  589.8 4.4 collective-permute-start.8
  590.8 5.2 copy-start.24
  594.3 2.7 copy-start.37
  598.6 2.8 copy-start.21
  612.4 2.9 copy-start.6
  612.4 2.9 copy-start.32
  612.4 2.9 copy-start.34
  644.1 5.0 copy-start.10
  644.1 5.0 copy-start.11
  644.1 5.0 copy-start.12
  644.2 5.0 copy-start.16
  644.2 5.0 copy-start.44
  644.2 5.0 copy-start.46
  644.2 5.0 copy-start.53
  644.2 5.0 copy-start.54
  649.1 10.6 %copy-start.3 = (f32[1,4096,128]{1,2,0:T(8,128)}, f32[1,4096,128]{1,2,0:T(8,128)S(1)}, u32[]{:S(2)}) copy-start(f32[1,4096,128]{1,2,0:T(8,128)S(1)} %get-tuple-element.31) | copy-start | bytes 6291460
  649.1 10.6 %copy-start.4 = (f32[1,4096,128]{1,2,0:T(8,128)}, f32[1,4096,128]{1,2,0:T(8,128)S(1)}, u32[]{:S(2)}) copy-start(f32[1,4096,128]{1,2,0:T(8,128)S(1)} %get-tuple-element.32) | copy-start | bytes 6291460
  651.0 9.6 %copy-start.1 = (f32[1,4096,128]{1,2,0:T(8,128)}, f32[1,4096,128]{1,2,0:T(8,128)S(1)}, u32[]{:S(2)}) copy-start(f32[1,4096,128]{1,2,0:T(8,128)S(1)} %get-tuple-element.34) | copy-start | bytes 6291460
  651.1 3.1 copy-start.28
  651.1 3.1 copy-start.29
  651.1 8.6 %collective-permute-start.11 = (f32[2,128,256]{1,2,0:T(8,128)S(1)}, f32[2,128,256]{1,2,0:T(8,128)S(1)}, u32[]{:S(2)}, u32[]{:S(2)}) collective-permute-start(f32[2,128,256]{1,2,0:T(8,128)S(1)} %fusion.109), channel_id=1, source_target_pairs={{0,16},{16,0},{1,17},{17,1},{2,18},{18,2},{3,19},{19,3},{4,20},{20... | collective-permute-start | bytes 786440 | tf_op jit(solution)/shard_map/ppermute | solution.py:89
  653.2 51.4 %collective-permute-start.2 = (f32[2,2048,128]{1,2,0:T(8,128)}, f32[2,2048,128]{1,2,0:T(8,128)}, u32[]{:S(2)}, u32[]{:S(2)}) collective-permute-start(f32[2,2048,128]{1,2,0:T(8,128)} %fusion.58), channel_id=1, source_target_pairs={{0,16},{16,0},{1,17},{17,1},{2,18},{18,2},{3,19},{19,3},{4,20},{20... | collective-permute-start | bytes 6291464 | tf_op jit(solution)/shard_map/ppermute | solution.py:89
  659.7 2.9 collective-permute-start.12
  660.5 4.4 copy-start.14
  660.5 4.4 copy-start.27
  660.5 4.4 copy-start.38
  660.5 4.4 copy-start.40
  660.6 4.3 collective-permute-start.13
  662.1 84.5 %collective-permute-start.3 = (f32[2,2048,128]{1,2,0:T(8,128)}, f32[2,2048,128]{1,2,0:T(8,128)}, u32[]{:S(2)}, u32[]{:S(2)}) collective-permute-start(f32[2,2048,128]{1,2,0:T(8,128)} %fusion.56), channel_id=1, source_target_pairs={{0,16},{16,0},{1,17},{17,1},{2,18},{18,2},{3,19},{19,3},{4,20},{20... | collective-permute-start | bytes 6291464 | tf_op jit(solution)/shard_map/ppermute | solution.py:89
  669.6 77.0 %copy-start.2 = (f32[1,4096,128]{1,2,0:T(8,128)S(1)}, f32[1,4096,128]{1,2,0:T(8,128)}, u32[]{:S(2)}) copy-start(f32[1,4096,128]{1,2,0:T(8,128)} %copy-done.1) | copy-start | bytes 6291460
  (12 other events, 20.3 us)

commit v3 on v2

--- a/solution.py
+++ b/solution.py
@@ -4,6 +4,7 @@
 import jax.numpy as jnp
 import numpy as np
 from jax import lax
+from jax.experimental.layout import Layout, with_layout_constraint
 from jax.sharding import PartitionSpec as P
 
 height_chirp = 1
@@ -134,21 +135,25 @@
     left, right = halo(measured, half_beam)
     wide_measured = jnp.concatenate([left, measured, right], axis=2)
 
-    def sources_of(strip, step):
-        strip = jnp.concatenate(ha_order(ha_trade(lambda to: strip)), axis=2)
-        left, right = halo(strip, reach)
-        strip = jnp.concatenate([left, strip, right], axis=2)
-        low_re, low_im = strip[0], strip[1]
-        power = wide_mask * (low_re * low_re + low_im * low_im)
-        ranged = jnp.dot(rmat, power, precision=EXACT)
-        misfit = jnp.dot(ranged, forward_band, precision=EXACT) - wide_measured[step]
-        spread_back = jnp.dot(misfit, back_band, precision=EXACT)
-        back = jnp.einsum("pr,pa->ra", own_rmat, spread_back, precision=EXACT)
-        weight = 2.0 * lax.dynamic_slice_in_dim(mask, slab * share, share, 0) * back
-        mine = [
-            lax.dynamic_slice(low, (slab * share, reach), (share, a_dev)) for low in (low_re, low_im)
-        ]
-        return jnp.stack([weight * mine[0], weight * mine[1]])
+    def sources_of(strips):
+        strips = jnp.concatenate(ha_order(ha_trade(lambda to: strips)), axis=3)
+        left, right = halo(strips, reach)
+        strips = jnp.concatenate([left, strips, right], axis=3)
+        result = []
+        for step in range(strips.shape[0]):
+            low_re, low_im = strips[step, 0], strips[step, 1]
+            power = wide_mask * (low_re * low_re + low_im * low_im)
+            ranged = jnp.dot(rmat, power, precision=EXACT)
+            misfit = jnp.dot(ranged, forward_band, precision=EXACT) - wide_measured[step]
+            spread_back = jnp.dot(misfit, back_band, precision=EXACT)
+            back = jnp.einsum("pr,pa->ra", own_rmat, spread_back, precision=EXACT)
+            weight = 2.0 * lax.dynamic_slice_in_dim(mask, slab * share, share, 0) * back
+            mine = [
+                lax.dynamic_slice(low, (slab * share, reach), (share, a_dev))
+                for low in (low_re, low_im)
+            ]
+            result.append(jnp.stack([weight * mine[0], weight * mine[1]]))
+        return jnp.stack(result)
 
     all_pick, all_terrain = gathered[0], gathered[1]
     height = iota((1, total_h), 1)
@@ -187,18 +192,25 @@
             part = part.reshape(2, h_first // n_ha, h_second, lanes)
             w_part = lax.dynamic_index_in_dim(w_in, (slab - shift) % n_ha, 3, False)
             tall = tall + jnp.einsum("ocka,cabq->okbq", w_part, part, precision=FAST)
-        tall = jnp.stack(cmul(tall, (tw_re, tw_im)))
+        tall, tw = lax.optimization_barrier((tall, (tw_re, tw_im)))
+        tall = jnp.stack(cmul(tall, tw))
         tall = jnp.einsum("ocjb,ckbq->kojq", w_second, tall, precision=FAST)
-        tall = tall.reshape(n_dev, own, 2, h_second, lanes)
-        return lax.all_to_all(tall, both, split_axis=0, concat_axis=0)
+        return tall.reshape(n_dev, own * 2 * h_second, lanes)
 
     sent = [send_chunk(chunk) for chunk in range(chunks)]
-    arrived = [to_rows(parts) for parts in sent]
+    arrived = []
+    for chunk, parts in enumerate(sent):
+        if chunk > 0:
+            parts, _ = lax.optimization_barrier((parts, tall))
+        tall = to_rows(parts)
+        arrived.append(lax.all_to_all(tall, both, split_axis=0, concat_axis=0))
     rows = 0.0
     for chunk, part in enumerate(arrived):
         span = slice(chunk * lanes, (chunk + 1) * lanes)
+        part = part.reshape(n_dev, own, 2, h_second, lanes)
         part = jnp.einsum("ocnp,pucjq->onujq", w_blocks, part, precision=FAST)
-        part = jnp.stack(cmul(part, (ty_re[..., span], ty_im[..., span])))
+        part, ty = lax.optimization_barrier((part, (ty_re[..., span], ty_im[..., span])))
+        part = jnp.stack(cmul(part, ty))
         rows = rows + jnp.einsum("ocmq,cnujq->onujm", w_cols[..., span], part, precision=FAST)
 
     def own_rows(table):
@@ -220,14 +232,20 @@
     )
     next_rows = jnp.stack(cmul(rows, cmul(bent, y_turn)))
 
-    def to_tall(chunk):
+    def to_tall(chunk, cells):
         span = slice(chunk * lanes, (chunk + 1) * lanes)
-        part = jnp.einsum("ocqm,cnujm->onujq", w_cols[:, :, span], next_rows, precision=FAST)
-        part = jnp.stack(cmul(part, (ty_re[..., span], ty_im[..., span])))
+        part = jnp.einsum("ocqm,cnujm->onujq", w_cols[:, :, span], cells, precision=FAST)
+        part, ty = lax.optimization_barrier((part, (ty_re[..., span], ty_im[..., span])))
+        part = jnp.stack(cmul(part, ty))
         part = jnp.einsum("ocpn,cnujq->puojq", w_blocks, part, precision=FAST)
-        return lax.all_to_all(part, both, split_axis=0, concat_axis=0)
-
-    returned = [to_tall(chunk) for chunk in range(chunks)]
+        return part.reshape(n_dev, own * 2 * h_second, lanes)
+
+    returned = []
+    for chunk in range(chunks):
+        if chunk > 0:
+            next_rows, _ = lax.optimization_barrier((next_rows, part))
+        part = to_tall(chunk, next_rows)
+        returned.append(lax.all_to_all(part, both, split_axis=0, concat_axis=0))
 
     n_low = -(-bottom // h_first)
     low_bend = tuple(
@@ -240,14 +258,16 @@
     low = low.transpose(0, 2, 3, 4, 1).reshape(2, own, n_low, n_dev, cols)
     low = lax.all_to_all(low.transpose(3, 0, 1, 2, 4), both, split_axis=0, concat_axis=0)
     low = low.transpose(1, 3, 0, 2, 4).reshape(2, n_low * h_first, cols)[:, :bottom]
-    first_sources = sources_of(low, 0)
 
     lasts = []
     outs = []
     for chunk, part in enumerate(returned):
+        if lasts:
+            part, _ = lax.optimization_barrier((part, lasts[-1]))
         part = part.reshape(h_first, 2, h_second, lanes)
         part = jnp.einsum("ocbj,kcjq->okbq", w_second, part, precision=FAST)
-        part = jnp.stack(cmul(part, (tw_re, tw_im)))
+        part, tw = lax.optimization_barrier((part, (tw_re, tw_im)))
+        part = jnp.stack(cmul(part, tw))
         part = jnp.einsum("ocak,ckbq->oabq", w_first, part, precision=FAST)
         part = part.reshape(2, total_h, lanes)
         col_start = slab * cols + chunk * lanes
@@ -259,15 +279,17 @@
         tall_bent = tuple(
             tall_ground * jnp.einsum("fh,fq->hq", t, tall_hot, precision=FAST) for t in bend
         )
+        tall_bent = tuple(with_layout_constraint(t, Layout((0, 1))) for t in tall_bent)
         last = jnp.stack(cmul(part, cmul(tall_bent, tall_y)))
+        last = with_layout_constraint(last, Layout((0, 1, 2)))
         lasts.append(last)
         outs.append(
             ha_order(ha_trade(lambda to: lax.dynamic_slice_in_dim(last, to * h_dev, h_dev, 1)))
         )
     strip = jnp.concatenate([last[:, :bottom] for last in lasts], axis=2)
-    second_sources = sources_of(strip, 1)
+    sources = sources_of(jnp.stack([low, strip]))
     out = jnp.concatenate([outs[j][i] for i in range(n_ha) for j in range(chunks)], axis=2)
-    return (out, jnp.stack([first_sources, second_sources]))
+    return (out, sources)
 
 
 def solution(mesh):

time: 765 us -> 757 us (0.990); the launches traced: 761 us -> 742 us
  waiting for transfers between devices: 435 us -> 333 us
  blocking collectives: 15.8 us -> 113 us
  local copies, waits for them, and re-layouts: 93 us -> 54.9 us
  other arithmetic: 54 us -> 69.3 us
  matrix products: 112 us -> 126 us
    all_to_all x0 -> x1, blocking collectives: none -> 97.4 us  [local(): returned.append(lax.all_to_all(part, both, split_axis=0, concat_axis=0))]
    all_to_all x4 -> x3, waiting for transfers between devices: 208 us -> 120 us  [the longest x1 60.4 us: local(): returned.append(lax.all_to_all(part, both, split_axis=0, concat_axis=0))]
    ppermute x4 -> x3, waiting for transfers between devices: 60.8 us -> 2.42 us  [halo(): lax.ppermute(head, axis, [((i + 1) % count, i) for i in range(count)])]
    ppermute x6 -> x5, waiting for transfers between devices: 166 us -> 210 us  [ha_trade(): parts.append(lax.ppermute(piece_for((slab + shift) % count), 'ha', pairs))]
    reshape x3 -> x0, local copies, waits for them, and re-layouts: 12.8 us -> none  [the longest x2 11.7 us: to_rows(): tall = tall.reshape(n_dev, own, 2, h_second, lanes)]
    another operation x1, other arithmetic: 1.11 us -> 12.3 us  [local(): next_rows = jnp.stack(cmul(rows, cmul(bent, y_turn)))]
    dot_general x2, matrix products: 20.6 us -> 9.74 us  [to_tall(): jnp.einsum('ocqm,cnujm->onujq', w_cols[:, :, span], cells, precision=FAST)]
    all_to_all x4 -> x3, starting transfers between devices: 32 us -> 22.4 us  [the longest x2 16.4 us: local(): arrived.append(lax.all_to_all(tall, both, split_axis=0, concat_axis=0))]
  transfers between devices with their start and end apart: 19 -> 15, of which waited for: 12 -> 8; matrix products, arithmetic and copies ran while one was open for 19% -> 25% of each run, Pallas kernels for 0% -> 0%
where the time goes in v3:
time: 757 us; the launch traced here: 742 us
  waiting for transfers between devices  333 us (44%)
  matrix products  126 us (17%)
  blocking collectives  113 us (15%)
  other arithmetic  69.3 us (9%)
  local copies, waits for them, and re-layouts  54.9 us (7%)
  starting transfers between devices  44 us (6%)
    ppermute x5, waiting for transfers between devices, ha_trade(): parts.append(lax.ppermute(piece_for((slab + shift) % count), 'ha', pairs))  210 us
    all_to_all x1, blocking collectives, local(): returned.append(lax.all_to_all(part, both, split_axis=0, concat_axis=0))  97.4 us
    all_to_all x1, waiting for transfers between devices, local(): returned.append(lax.all_to_all(part, both, split_axis=0, concat_axis=0))  60.4 us
    all_to_all x2, waiting for transfers between devices, local(): arrived.append(lax.all_to_all(tall, both, split_axis=0, concat_axis=0))  60.1 us
    sub x10, other arithmetic, cmul(): left[0] * right[0] - left[1] * right[1]  17.4 us
    all_to_all x2, starting transfers between devices, local(): arrived.append(lax.all_to_all(tall, both, split_axis=0, concat_axis=0))  16.4 us
    all_gather x1, blocking collectives, local(): lax.all_gather(jnp.stack([profile_pick, terrain]), 'az', axis=1, tiled=True)  15.8 us
    dot_general x2, matrix products, local(): part = jnp.einsum('ocnp,pucjq->onujq', w_blocks, part, precision=FAST)  15.3 us
  transfers between devices with their start and end apart: 15, of which 8 were waited for; matrix products, arithmetic and copies ran while one was open for 25% of the time, Pallas kernels for 0%

profile of v3, /device:TPU:11, one launch (start us, length us, event | category | flops | bytes accessed | tf_op | source)
XLA Modules:
  0.0 742.5 jit_solution(11661448370715063181)
XLA Ops:
  1.6 15.8 %all_gather.3 = s32[2,8192]{1,0:T(2,128)S(1)} all-gather(s32[2,512]{1,0:T(2,128)S(1)} %pad_add_fusion), channel_id=1, replica_groups=mesh['ha'=2,'az'=16] {'az'}, dimensions={1}, use_global_device_ids=true | all-gather | bytes 69632 | tf_op jit(solution)/shard_map/all_gather | solution.py:107
  17.4 4.4 slice_bitcast_fusion.2
  25.2 1.4 pad_maximum_fusion.5
  27.9 2.6 multiply_subtract_fusion.14
  32.5 1.9 fusion.59
  34.4 39.6 %collective-permute-done = f32[2,2048,128]{2,1,0:T(8,128)} collective-permute-done((f32[2,2048,128]{2,1,0:T(8,128)}, f32[2,2048,128]{2,1,0:T(8,128)}, u32[]{:S(2)}, u32[]{:S(2)}) %collective-permute-start) | collective-permute-done | bytes 2097184 | tf_op jit(solution)/shard_map/ppermute | solution.py:90
  74.1 4.5 bitcast_add_fusion.2
  80.5 7.4 fusion.23
  87.9 11.3 %all-to-all-start = ((f32[32,256,128]{2,1,0:T(8,128)}), f32[32,256,128]{2,1,0:T(8,128)}, u32[]{:S(2)}, u32[]{:S(2)}) async-start(f32[32,256,128]{2,1,0:T(8,128)} %bitcast.516), calls=%async_computation | async-start | bytes 8388608 | tf_op jit(solution)/shard_map/all_to_all | solution.py:206
  99.3 2.7 subtract_bitcast_fusion.1
  105.3 86.1 %collective-permute-done.1 = f32[2,2048,128]{2,1,0:T(8,128)S(1)} collective-permute-done((f32[2,2048,128]{2,1,0:T(8,128)S(1)}, f32[2,2048,128]{2,1,0:T(8,128)S(1)}, u32[]{:S(2)}, u32[]{:S(2)}) %collective-permute-start.1) | collective-permute-done | bytes 2097184 | tf_op jit(solution)/shard_map/ppermute | solution.py:90
  191.3 2.9 fusion.67
  194.3 3.0 bitcast_add_fusion.1
  199.3 7.3 fusion.17
  206.6 5.1 all-to-all-start.1
  215.0 1.9 copy.161
  217.6 2.0 copy.141
  220.5 2.0 copy.139
  228.7 1.5 broadcast_compare_fusion
  230.6 3.4 fusion.90
  234.0 8.4 %fusion.31 = f32[2,32,2,64,128]{4,1,3,2,0:T(8,128)} fusion(f32[32,2,2,64,128]{4,3,2,1,0:T(8,128)} %bitcast.40, f32[1,2,32,32]{3,2,1,0:T(8,128)S(1)} %get-tuple-element.134, f32[1,2,32,32]{3,2,1,0:T(8,128)S(1)} %get-tuple-element.133), kind=kOutput, calls=%fused_computation.73 | convolution fusion | flops 402657280 | bytes 8404992 | tf_op jit(solution)/shard_map/ocnp,pucjq->onujq/dot_general | solution.py:211
  242.3 60.1 %all-to-all-done.1 = f32[32,256,128]{2,1,0:T(8,128)} async-done(((f32[32,256,128]{2,1,0:T(8,128)}), f32[32,256,128]{2,1,0:T(8,128)}, u32[]{:S(2)}, u32[]{:S(2)}) %all-to-all-start.1) | async-done | bytes 4194336 | tf_op jit(solution)/shard_map/all_to_all | solution.py:206
  302.4 6.9 fusion.34
  311.8 6.6 fusion.13
  318.4 6.9 fusion.4
  325.3 3.4 copy-done.12
  331.7 7.2 all-to-all-start.4
  339.0 8.5 %subtract_bitcast_fusion = (f32[1,32,2,64,256]{4,3,2,1,0:T(8,128)}, f32[1,32,2,64,256]{4,3,2,1,0:T(8,128)}) fusion(f32[2,32,2,64,256]{4,3,0,2,1:T(8,128)} %copy-done.12, f32[32,256]{1,0:T(8,128)S(1)} %get-tuple-element.149, f32[32,256,2,64]{1,3,2,0:T(8,128)} %fusion.90, f32[32,256]{1,0:T(8,128)S(1)} %get-tuple-element.148, s32[32,256]{1,0:T(8,128)S(1)} %copy-done.37, ...), kind=kOutput, calls=%fused_computation.66 | convolution fusion | flops 116523008 | bytes 21111296 | tf_op jit(solution)/shard_map/fuj,fnm->nujm/dot_general | solution.py:231
  347.5 12.3 %fusion.284 = (f32[2,32,2,64,256,1]{4,3,2,1,0,5:T(8,128)}, f32[2,32,2,64,256]{4,3,2,1,0:T(8,128)}) fusion(f32[1,32,2,64,256]{4,3,2,1,0:T(8,128)} %get-tuple-element.68, f32[1,32,2,64,256]{4,3,2,1,0:T(8,128)} %get-tuple-element.67), kind=kLoop, calls=%fused_computation.530 | loop fusion | flops 2097152 | bytes 25165824 | tf_op jit(solution)/shard_map/stack | solution.py:233
  359.8 6.3 fusion.49
  367.7 4.3 fusion.37
  372.0 4.5 copy.146
  376.5 3.5 fusion.52
  381.5 4.3 fusion.43
  385.8 4.4 copy.154
  390.3 97.4 %all_to_all.25 = f32[32,256,128]{2,1,0:T(8,128)} all-to-all(f32[32,256,128]{2,1,0:T(8,128)} %bitcast.517), channel_id=1, replica_groups=mesh['ha'=2,'az'=16] {'az','ha'}, dimensions={0} | all-to-all | bytes 8388608 | tf_op jit(solution)/shard_map/all_to_all | solution.py:248
  487.7 5.9 all-to-all-start.2
  497.5 2.6 collective-permute-start.9
  502.5 2.6 convolution_select_fusion.1
  505.1 2.6 convolution_select_fusion.3
  507.8 4.4 select_reduce_fusion.1
  512.2 4.6 select_reduce_fusion
  517.8 6.2 convolution_bitcast_fusion
  524.0 60.4 %all-to-all-done.2 = f32[32,256,128]{2,1,0:T(8,128)} async-done(((f32[32,256,128]{2,1,0:T(8,128)}), f32[32,256,128]{2,1,0:T(8,128)}, u32[]{:S(2)}, u32[]{:S(2)}) %all-to-all-start.2) | async-done | bytes 4194336 | tf_op jit(solution)/shard_map/all_to_all | solution.py:248
  584.4 6.0 convolution_bitcast_fusion.1
  590.5 3.6 multiply_subtract_fusion.5
  594.7 4.2 fusion.40
  599.5 2.5 copy.150
  602.0 1.5 copy.155
  603.5 1.4 copy.156
  604.9 4.0 multiply_subtract_fusion.2
  609.8 4.1 fusion.46
  619.2 1.9 fusion.65
  623.5 2.1 fusion.63
  628.5 1.6 collective-permute-start.6
  631.7 1.7 fusion.56
  633.5 8.1 %collective-permute-done.6 = f32[2,2,128,256]{3,2,1,0:T(8,128)} collective-permute-done((f32[2,2,128,256]{3,2,1,0:T(8,128)}, f32[2,2,128,256]{3,2,1,0:T(8,128)}, u32[]{:S(2)}, u32[]{:S(2)}) %collective-permute-start.6) | collective-permute-done | bytes 524320 | tf_op jit(solution)/shard_map/ppermute | solution.py:90
  642.8 1.8 collective-permute-start.8
  647.7 2.4 collective-permute-done.8
  652.1 1.8 fusion.94
  656.6 1.7 fusion.95
  661.8 31.6 %collective-permute-done.2 = f32[2,2048,128]{2,1,0:T(8,128)S(1)} collective-permute-done((f32[2,2048,128]{2,1,0:T(8,128)S(1)}, f32[2,2048,128]{2,1,0:T(8,128)S(1)}, u32[]{:S(2)}, u32[]{:S(2)}) %collective-permute-start.2) | collective-permute-done | bytes 2097184 | tf_op jit(solution)/shard_map/ppermute | solution.py:90
  693.6 44.7 %collective-permute-done.3 = f32[2,2048,128]{2,1,0:T(8,128)S(1)} collective-permute-done((f32[2,2048,128]{2,1,0:T(8,128)S(1)}, f32[2,2048,128]{2,1,0:T(8,128)S(1)}, u32[]{:S(2)}, u32[]{:S(2)}) %collective-permute-start.3) | collective-permute-done | bytes 2097184 | tf_op jit(solution)/shard_map/ppermute | solution.py:90
  738.6 3.7 pad_maximum_fusion.1
  (241 shorter events, 68.7 us)
Async XLA Ops:
  21.8 2.0 copy-start
  21.8 3.4 copy-start.2
  26.7 47.4 %collective-permute-start = (f32[2,2048,128]{2,1,0:T(8,128)}, f32[2,2048,128]{2,1,0:T(8,128)}, u32[]{:S(2)}, u32[]{:S(2)}) collective-permute-start(f32[2,2048,128]{2,1,0:T(8,128)} %pad_maximum_fusion.5), channel_id=1, source_target_pairs={{0,16},{16,0},{1,17},{17,1},{2,18},{18,2},{3,19},{19,3},{4,20},{20... | collective-permute-start | bytes 6291464 | tf_op jit(solution)/shard_map/ppermute | solution.py:90
  32.2 165.0 %copy-start.28 = (f32[64,64,1]{0,1,2:T(8,128)}, f32[64,64,1]{0,1,2:T(8,128)S(1)}, u32[]{:S(2)}) copy-start(f32[64,64,1]{0,1,2:T(8,128)S(1)} %get-tuple-element.53) | copy-start | bytes 49156
  32.2 165.0 %copy-start.30 = (f32[64,64,1]{0,1,2:T(8,128)}, f32[64,64,1]{0,1,2:T(8,128)S(1)}, u32[]{:S(2)}) copy-start(f32[64,64,1]{0,1,2:T(8,128)S(1)} %get-tuple-element.52) | copy-start | bytes 49156
  32.3 167.0 %copy-start.20 = (f32[1,2,64,64]{3,2,1,0:T(8,128)}, f32[1,2,64,64]{3,2,1,0:T(8,128)S(1)}, u32[]{:S(2)}) copy-start(f32[1,2,64,64]{3,2,1,0:T(8,128)S(1)} %get-tuple-element.132) | copy-start | bytes 98308
  87.9 118.7 %all-to-all-start = ((f32[32,256,128]{2,1,0:T(8,128)}), f32[32,256,128]{2,1,0:T(8,128)}, u32[]{:S(2)}, u32[]{:S(2)}) async-start(f32[32,256,128]{2,1,0:T(8,128)} %bitcast.516), calls=%async_computation | async-start | bytes 8388608 | tf_op jit(solution)/shard_map/all_to_all | solution.py:206
  99.3 4.2 copy-start.3
  102.0 2.4 copy-start.1
  102.2 89.2 %collective-permute-start.1 = (f32[2,2048,128]{2,1,0:T(8,128)S(1)}, f32[2,2048,128]{2,1,0:T(8,128)S(1)}, u32[]{:S(2)}, u32[]{:S(2)}) collective-permute-start(f32[2,2048,128]{2,1,0:T(8,128)S(1)} %pad_maximum_fusion.7), channel_id=1, source_target_pairs={{0,16},{16,0},{1,17},{17,1},{2,18},{18,2},{3,19},{19,3},{4,20},{20... | collective-permute-start | bytes 6291464 | tf_op jit(solution)/shard_map/ppermute | solution.py:90
  206.6 7.1 copy-start.33
  206.6 95.8 %all-to-all-start.1 = ((f32[32,256,128]{2,1,0:T(8,128)}), f32[32,256,128]{2,1,0:T(8,128)}, u32[]{:S(2)}, u32[]{:S(2)}) async-start(f32[32,256,128]{2,1,0:T(8,128)} %bitcast.513), calls=%async_computation.1 | async-start | bytes 8388608 | tf_op jit(solution)/shard_map/all_to_all | solution.py:206
  215.0 2.5 copy-start.16
  225.7 4.5 copy-start.36
  302.4 6.9 copy-start.10
  325.3 3.4 copy-start.12
  330.0 8.9 %copy-start.37 = (s32[32,256]{1,0:T(8,128)S(1)}, s32[32,256]{1,0:T(8,128)}, u32[]{:S(2)}) copy-start(s32[32,256]{1,0:T(8,128)} %copy.137) | copy-start | bytes 98308
  330.0 8.9 %copy-start.38 = (f32[16,64,1,2]{1,0,3,2:T(8,128)S(1)}, f32[16,64,1,2]{1,0,3,2:T(8,128)}, u32[]{:S(2)}) copy-start(f32[16,64,1,2]{1,0,3,2:T(8,128)} %copy.140) | copy-start | bytes 24580
  331.7 58.5 %all-to-all-start.4 = ((f32[32,2,2,2,256]{4,3,2,1,0:T(2,128)}), f32[32,2,2,2,256]{4,3,2,1,0:T(2,128)S(1)}, u32[]{:S(2)}, u32[]{:S(2)}) async-start(f32[32,2,2,2,256]{4,3,2,1,0:T(2,128)} %copy.166), calls=%async_computation.4 | async-start | bytes 524288 | tf_op jit(solution)/shard_map/all_to_all | solution.py:259
  367.0 9.4 %slice-start = ((s8[8388608]{0:T(1024)(128)(4,1)}), s8[4194304]{0:T(1024)(128)(4,1)S(1)}, s32[]{:S(2)}) async-start(s8[8388608]{0:T(1024)(128)(4,1)} %bitcast.499), calls=%async_computation.5 | async-start | bytes 8388608
  367.6 8.8 %slice-start.1 = ((s8[8388608]{0:T(1024)(128)(4,1)}), s8[4194304]{0:T(1024)(128)(4,1)S(1)}, s32[]{:S(2)}) async-start(s8[8388608]{0:T(1024)(128)(4,1)} %bitcast.499), calls=%async_computation.6 | async-start | bytes 8388608
  487.7 6.0 copy-start.34
  487.7 8.9 %copy-start.32 = (f32[2,128,512]{2,1,0:T(8,128)S(1)}, f32[2,128,512]{2,1,0:T(8,128)}, u32[]{:S(2)}) copy-start(f32[2,128,512]{2,1,0:T(8,128)} %param.15) | copy-start | bytes 1572868
  487.7 13.8 %copy-start.39 = (s32[512]{0:T(512)S(1)}, s32[512]{0:T(512)}, u32[]{:S(2)}) copy-start(s32[512]{0:T(512)} %param.9) | copy-start | bytes 6148
  487.7 13.8 %copy-start.40 = (s32[512]{0:T(512)S(1)}, s32[512]{0:T(512)}, u32[]{:S(2)}) copy-start(s32[512]{0:T(512)} %param.10) | copy-start | bytes 6148
  487.7 96.6 %all-to-all-start.2 = ((f32[32,256,128]{2,1,0:T(8,128)}), f32[32,256,128]{2,1,0:T(8,128)}, u32[]{:S(2)}, u32[]{:S(2)}) async-start(f32[32,256,128]{2,1,0:T(8,128)} %bitcast.514), calls=%async_computation.2 | async-start | bytes 8388608 | tf_op jit(solution)/shard_map/all_to_all | solution.py:248
  495.2 156.9 %collective-permute-start.4 = (f32[128,30]{1,0:T(8,128)}, f32[128,30]{1,0:T(8,128)}, u32[]{:S(2)}, u32[]{:S(2)}) collective-permute-start(f32[128,30]{1,0:T(8,128)} %get-tuple-element.119), channel_id=1, source_target_pairs={{0,1},{1,2},{2,3},{3,4},{4,5},{5,6},{6,7},{7,8},{8,9},{9,10},{10,1... | collective-permute-start | bytes 46088 | tf_op jit(solution)/shard_map/ppermute | solution.py:72
  496.6 155.5 %collective-permute-start.5 = (f32[128,30]{1,0:T(8,128)}, f32[128,30]{1,0:T(8,128)}, u32[]{:S(2)}, u32[]{:S(2)}) collective-permute-start(f32[128,30]{1,0:T(8,128)} %get-tuple-element.120), channel_id=1, source_target_pairs={{1,0},{2,1},{3,2},{4,3},{5,4},{6,5},{7,6},{8,7},{9,8},{10,9},{11,1... | collective-permute-start | bytes 46088 | tf_op jit(solution)/shard_map/ppermute | solution.py:73
  496.8 8.3 %copy-start.27 = (f32[2,128,512]{1,2,0:T(8,128)}, f32[2,128,512]{1,2,0:T(8,128)S(1)}, u32[]{:S(2)}) copy-start(f32[2,128,512]{1,2,0:T(8,128)S(1)} %copy.168) | copy-start | bytes 1572868
  497.5 133.1 %collective-permute-start.9 = (f32[2,128,15]{1,2,0:T(8,128)}, f32[2,128,15]{1,2,0:T(8,128)}, u32[]{:S(2)}, u32[]{:S(2)}) collective-permute-start(f32[2,128,15]{1,2,0:T(8,128)} %get-tuple-element.117), channel_id=1, source_target_pairs={{0,1},{1,2},{2,3},{3,4},{4,5},{5,6},{6,7},{7,8},{8,9},{9,10},{10,1... | collective-permute-start | bytes 46088 | tf_op jit(solution)/shard_map/ppermute | solution.py:72
  500.1 130.5 %collective-permute-start.10 = (f32[2,128,15]{1,2,0:T(8,128)}, f32[2,128,15]{1,2,0:T(8,128)}, u32[]{:S(2)}, u32[]{:S(2)}) collective-permute-start(f32[2,128,15]{1,2,0:T(8,128)} %get-tuple-element.118), channel_id=1, source_target_pairs={{1,0},{2,1},{3,2},{4,3},{5,4},{6,5},{7,6},{8,7},{9,8},{10,9},{11,1... | collective-permute-start | bytes 46088 | tf_op jit(solution)/shard_map/ppermute | solution.py:73
  501.6 3.5 copy-start.41
  501.6 3.5 copy-start.43
  501.6 3.5 copy-start.45
  501.6 3.5 copy-start.47
  502.5 5.3 copy-start.49
  512.2 5.6 copy-start.21
  584.4 6.0 copy-start.31
  584.4 6.1 copy-start.29
  615.7 2.5 copy-start.17
  617.0 2.2 copy-start.15
  617.0 2.2 copy-start.46
  617.0 2.2 copy-start.48
  617.0 2.2 copy-start.53
  617.0 2.2 copy-start.54
  621.1 2.3 copy-start.13
  621.1 2.3 copy-start.42
  621.2 2.3 copy-start.44
  621.2 2.3 copy-start.51
  621.2 2.3 copy-start.52
  625.6 4.5 copy-start.35
  625.6 4.5 copy-start.50
  628.5 13.1 %collective-permute-start.6 = (f32[2,2,128,256]{3,2,1,0:T(8,128)}, f32[2,2,128,256]{3,2,1,0:T(8,128)}, u32[]{:S(2)}, u32[]{:S(2)}) collective-permute-start(f32[2,2,128,256]{3,2,1,0:T(8,128)} %pad_maximum_fusion.11), channel_id=1, source_target_pairs={{0,16},{16,0},{1,17},{17,1},{2,18},{18,2},{3,19},{19,3},{4,20},{20... | collective-permute-start | bytes 1572872 | tf_op jit(solution)/shard_map/ppermute | solution.py:90
  631.7 9.8 %copy-start.24 = (f32[1,2,128,256]{3,2,1,0:T(8,128)S(1)}, f32[1,2,128,256]{3,2,1,0:T(8,128)}, u32[]{:S(2)}) copy-start(f32[1,2,128,256]{3,2,1,0:T(8,128)} %copy-done.23) | copy-start | bytes 786436
  631.7 9.8 %copy-start.26 = (f32[1,2,128,256]{3,2,1,0:T(8,128)S(1)}, f32[1,2,128,256]{3,2,1,0:T(8,128)}, u32[]{:S(2)}) copy-start(f32[1,2,128,256]{3,2,1,0:T(8,128)} %stack_reshape.3) | copy-start | bytes 786436
  633.4 12.6 %copy-start.5 = (f32[4096,128]{1,0:T(8,128)S(1)}, f32[4096,128]{1,0:T(8,128)}, u32[]{:S(2)}) copy-start(f32[4096,128]{1,0:T(8,128)} %copy-done.4) | copy-start | bytes 6291460
  642.8 7.3 collective-permute-start.8
  644.6 6.9 collective-permute-start.7
  646.3 5.8 copy-start.19
  646.3 47.1 %collective-permute-start.2 = (f32[2,2048,128]{2,1,0:T(8,128)S(1)}, f32[2,2048,128]{2,1,0:T(8,128)S(1)}, u32[]{:S(2)}, u32[]{:S(2)}) collective-permute-start(f32[2,2048,128]{2,1,0:T(8,128)S(1)} %fusion.57), channel_id=1, source_target_pairs={{0,16},{16,0},{1,17},{17,1},{2,18},{18,2},{3,19},{19,3},{4,20},{20... | collective-permute-start | bytes 6291464 | tf_op jit(solution)/shard_map/ppermute | solution.py:90
  650.1 88.2 %collective-permute-start.3 = (f32[2,2048,128]{2,1,0:T(8,128)S(1)}, f32[2,2048,128]{2,1,0:T(8,128)S(1)}, u32[]{:S(2)}, u32[]{:S(2)}) collective-permute-start(f32[2,2048,128]{2,1,0:T(8,128)S(1)} %fusion.56), channel_id=1, source_target_pairs={{0,16},{16,0},{1,17},{17,1},{2,18},{18,2},{3,19},{19,3},{4,20},{20... | collective-permute-start | bytes 6291464 | tf_op jit(solution)/shard_map/ppermute | solution.py:90
  652.1 3.1 copy-start.11
  661.8 76.5 %copy-start.7 = (f32[4096,128]{1,0:T(8,128)S(1)}, f32[4096,128]{1,0:T(8,128)}, u32[]{:S(2)}) copy-start(f32[4096,128]{1,0:T(8,128)} %copy-done.6) | copy-start | bytes 6291460
  661.8 76.5 %copy-start.9 = (f32[4096,128]{1,0:T(8,128)S(1)}, f32[4096,128]{1,0:T(8,128)}, u32[]{:S(2)}) copy-start(f32[4096,128]{1,0:T(8,128)} %copy-done.8) | copy-start | bytes 6291460
  (8 other events, 10.7 us)
